TPU v7x, 512 devices: a whole 4x8x8 slice. The times are simulated.
512 devices in a mesh: inst: 8 (over y), space: 64 (over x, z, core).
Axes of the slice: x: 4, y: 8, z: 8, core: 2. Of those that a mesh axis runs over, the one named last changes fastest.
Arguments:
- adjoint: float32 [16, 5, 8192, 128], P('inst', None, 'space'), may hold values from -6 to 6
- source: float32 [16, 5, 8192, 128], P('inst', None, 'space'), may hold values from -6 to 6
- coefficient: float32 [5, 8192, 128], P(None, 'space'), may hold values from 0.2 to 2
- volume: float32 [8192, 128], P('space'), may hold values from 0.5 to 2
- mixing: float32 [5, 5, 5], replicated, may hold values from -2.5 to 2.5
- face_partner: int32 [16, 256], P('inst'), may hold values from 0 to 255, as said below
Outputs:
- residual: float32 [16, 5, 8192, 128], P('inst', None, 'space')
Inputs may be any that keep to these rules, and one draw needn't show every extreme that they name: `face_partner`: for each instance n there is a rotation s_n = 4 * k_n + e_n with k_n in 1 to 30 and e_n in 1 to 3. A global block x = 4 * p + b (sector j = p // 2) has index j * 4 + b within its blade row; a rotor block of index G is paired with the stator block of index (G + s_n) mod 128, a stator block of index G with the rotor block of index (G - s_n) mod 128; the partner of index H lies on device 2 * (H // 4) plus 1 for a stator partner, as block H mod 4.
All inputs are finite; a program needn't handle non-finite values.
Results may differ from a plain program's by a relative error of at most 0.000059.
Values sent between devices are 32-bit elements; how exact they have to be, the bound alone decides.
A program may use at most 64 MiB of HBM per device.

v0:
```python
import jax
import jax.numpy as jnp
from jax import lax
from jax.sharding import PartitionSpec as P

NI = 16
NB = 4
FB = 32


highest = lax.Precision.HIGHEST
spin_rate = 0.75


def from_behind(value, axis, steps):
    count = lax.axis_size(axis)
    pairs = [(source, (source + steps) % count) for source in range(count)]
    return lax.ppermute(value, axis, pairs)


def swapped(value, axis, apart):
    mask = 2**apart
    pairs = [(source, source ^ mask) for source in range(lax.axis_size(axis))]
    return lax.ppermute(value, axis, pairs)


def spectral_matrix(inst_count):
    inst_order = jnp.arange(inst_count)
    offset = inst_order[:, None] - inst_order[None, :]
    angle_value = jnp.pi * offset.astype(jnp.float32) / inst_count
    parity = jnp.where(offset % 2 == 0, 1.0, -1.0).astype(jnp.float32)
    sine_value = jnp.where(offset == 0, 1.0, jnp.sin(angle_value))
    return jnp.where(offset == 0, 0.0, 0.5 * parity * jnp.cos(angle_value) / sine_value)


def mix(matrix, grid_field):
    return jnp.einsum("uv,nuar->nvar", matrix, grid_field, precision=highest)


def local(adjoint, source, coefficient, volume, mixing, face_partner):
    inst_dev, nvar, cells_a, cells_r = adjoint.shape
    center = mix(mixing[0], coefficient[0][None, None] * adjoint)
    ahead = coefficient[1][None, None] * adjoint
    behind = coefficient[2][None, None] * adjoint
    outward = coefficient[3][None, None] * adjoint
    inward = coefficient[4][None, None] * adjoint
    from_prev = from_behind(ahead[:, :, cells_a - 1 :, :], "space", 2)
    from_next = from_behind(behind[:, :, :1, :], "space", -2)
    ahead_moved = jnp.concatenate([from_prev, ahead[:, :, :-1, :]], axis=2)
    behind_moved = jnp.concatenate([behind[:, :, 1:, :], from_next], axis=2)
    face_rows = outward[:, :, :, cells_r - 1]
    is_rotor = lax.axis_index("space") % 2 == 0
    held_face = swapped(face_rows, "space", 0)
    next_held = from_behind(held_face, "space", -2)
    window = jnp.concatenate([held_face, next_held], axis=2)
    sectors = lax.axis_size("space") // 2
    half_count = sectors * NB
    first_partner = face_partner[:, 0]
    rotation = first_partner // NB // 2 * NB + first_partner % NB
    forward = jnp.where(is_rotor, rotation, half_count - rotation)
    sector_shift = forward // NB
    block_shift = forward % NB
    for bit_index in range((sectors - 1).bit_length()):
        upward = from_behind(window, "space", -(2 << bit_index))
        bit_set = (sector_shift >> bit_index) % 2 == 1
        window = jnp.where(bit_set[:, None, None], upward, window)
    window_slots = window.reshape(inst_dev, nvar, 2 * NB, FB)
    own_block = jnp.arange(NB, dtype=jnp.int32)[None, :]
    position = own_block + block_shift[:, None]
    chosen = (position[:, :, None] == jnp.arange(2 * NB, dtype=jnp.int32)[None, None, :]).astype(
        jnp.float32
    )
    received = jnp.einsum("ibk,ivkf->ivbf", chosen, window_slots, precision=highest).reshape(
        inst_dev, nvar, cells_a
    )
    zero_column = jnp.zeros_like(outward[:, :, :, :1])
    radial_moved = (
        jnp.concatenate([zero_column, outward[:, :, :, :-1]], axis=3)
        .at[:, :, :, cells_r - 1]
        .add(received)
    )
    inward_moved = jnp.concatenate([inward[:, :, :, 1:], zero_column], axis=3)
    spec_table = spectral_matrix(NI)
    turned = jnp.einsum(
        "mn,mvar->nvar",
        spec_table,
        lax.all_to_all(adjoint, "inst", split_axis=2, concat_axis=0, tiled=True),
        precision=highest,
    )
    spectral = lax.all_to_all(turned, "inst", split_axis=0, concat_axis=2, tiled=True)
    total = source + center + mix(mixing[1], ahead_moved) + mix(mixing[2], behind_moved)
    total = total + mix(mixing[3], radial_moved) + mix(mixing[4], inward_moved)
    return total + spin_rate * volume[None, None] * spectral


def solution(mesh):
    in_specs = (
        P("inst", None, "space", None),
        P("inst", None, "space", None),
        P(None, "space", None),
        P("space", None),
        P(),
        P("inst", None),
    )
    out_specs = P("inst", None, "space", None)
    return jax.shard_map(local, mesh=mesh, in_specs=in_specs, out_specs=out_specs, check_vma=False)
```

profile of v0, /device:TPU:198, one launch (start us, length us, event | category | flops | bytes accessed | tf_op | source)
XLA Modules:
  0.0 105.1 jit_solution(5381021497391826725)
XLA Ops:
  0.0 1.1 %slice_bitcast_fusion = (f32[128,128]{1,0:T(8,128)S(1)}, f32[128,128]{1,0:T(8,128)S(1)}, f32[128,128]{1,0:T(8,128)S(1)}, f32[128,128]{1,0:T(8,128)S(1)}, f32[128,128]{1,0:T(8,128)S(1)}) fusion(f32[5,128,128]{2,1,0:T(8,128)} %param.10), kind=kLoop, calls=%fused_computation.25 | loop fusion | bytes 655360 | tf_op jit(solution)/shard_map/mul | solution.py:46
  1.2 0.8 copy.48
  2.4 1.9 %collective-permute-start.2 = (f32[2,5,128]{2,0,1:T(2,128)S(1)}, f32[2,5,128]{2,0,1:T(2,128)S(1)}, u32[]{:S(2)}, u32[]{:S(2)}) collective-permute-start(f32[2,5,128]{2,0,1:T(2,128)S(1)} %slice_bitcast_fusion.5), channel_id=1, source_target_pairs={{0,1},{1,0},{2,3},{3,2},{4,5},{5,4},{6,7},{7,6},{8,9},{9,8},{10,11... | collective-permute-start | bytes 15368 | tf_op jit(solution)/shard_map/ppermute | solution.py:24
  4.8 1.9 %collective-permute-start.1 = (f32[2,5,1,128]{3,1,2,0:T(8,128)S(1)}, f32[2,5,1,128]{3,1,2,0:T(8,128)S(1)}, u32[]{:S(2)}, u32[]{:S(2)}) collective-permute-start(f32[2,5,1,128]{3,1,2,0:T(8,128)S(1)} %slice.105), channel_id=1, source_target_pairs={{0,62},{1,63},{2,0},{3,1},{4,2},{5,3},{6,4},{7,5},{8,6},{9,7},{10,... | collective-permute-start | bytes 15368 | tf_op jit(solution)/shard_map/ppermute | solution.py:18
  6.8 5.5 %collective-permute-start = (f32[2,5,1,128]{3,1,2,0:T(8,128)S(1)}, f32[2,5,1,128]{3,1,2,0:T(8,128)S(1)}, u32[]{:S(2)}, u32[]{:S(2)}) collective-permute-start(f32[2,5,1,128]{3,1,2,0:T(8,128)S(1)} %slice.102), channel_id=1, source_target_pairs={{0,2},{1,3},{2,4},{3,5},{4,6},{5,7},{6,8},{7,9},{8,10},{9,11},{10,... | collective-permute-start | bytes 15368 | tf_op jit(solution)/shard_map/ppermute | solution.py:18
  12.3 1.4 %copy.55 = f32[2,5,128,128]{3,1,0,2:T(8,128)} copy(f32[2,5,128,128]{3,2,1,0:T(8,128)S(1)} %copy-done) | data formatting | bytes 1310720 | tf_op args[0]
  13.6 7.1 %all-to-all-start = ((f32[2,5,128,128]{3,1,0,2:T(8,128)}), f32[2,5,128,128]{3,1,0,2:T(8,128)S(1)}, u32[]{:S(2)}, u32[]{:S(2)}) async-start(f32[2,5,128,128]{3,1,0,2:T(8,128)} %copy.55), calls=%async_computation | async-start | bytes 2097152 | tf_op jit(solution)/shard_map/all_to_all | solution.py:87
  22.8 1.7 %fusion.5 = f32[2,5,128,128]{3,1,2,0:T(8,128)S(1)} fusion(f32[2,5,128,128]{3,2,1,0:T(8,128)S(1)} %copy-done.9, f32[2,5,128,128]{3,2,1,0:T(8,128)S(1)} %broadcast_multiply_fusion.3, f32[5,5,5]{2,1,0:T(8,128)S(1)} %copy-done.11), kind=kOutput, calls=%fused_computation.10 | convolution fusion | flops 9994240 | bytes 1970176 | tf_op jit(solution)/shard_map/uv,nuar->nvar/dot_general | solution.py:37
  24.5 2.1 %collective-permute-start.3 = (f32[2,5,128]{2,0,1:T(2,128)S(1)}, f32[2,5,128]{2,0,1:T(2,128)S(1)}, u32[]{:S(2)}, u32[]{:S(2)}) collective-permute-start(f32[2,5,128]{2,0,1:T(2,128)S(1)} %collective-permute-done.2), channel_id=1, source_target_pairs={{0,62},{1,63},{2,0},{3,1},{4,2},{5,3},{6,4},{7,5},{8,6},{9,7},{10,... | collective-permute-start | bytes 15368 | tf_op jit(solution)/shard_map/ppermute | solution.py:18
  26.6 4.8 %collective-permute-done.3 = f32[2,5,128]{2,0,1:T(2,128)S(1)} collective-permute-done((f32[2,5,128]{2,0,1:T(2,128)S(1)}, f32[2,5,128]{2,0,1:T(2,128)S(1)}, u32[]{:S(2)}, u32[]{:S(2)}) %collective-permute-start.3) | collective-permute-done | bytes 5152 | tf_op jit(solution)/shard_map/ppermute | solution.py:18
  31.3 1.9 %collective-permute-start.4 = (f32[2,5,256]{2,0,1:T(2,128)S(1)}, f32[2,5,256]{2,0,1:T(2,128)S(1)}, u32[]{:S(2)}, u32[]{:S(2)}) collective-permute-start(f32[2,5,256]{2,0,1:T(2,128)S(1)} %constant_dynamic-update-slice_fusion), channel_id=1, source_target_pairs={{0,62},{1,63},{2,0},{3,1},{4,2},{5,3},{6,4},{7,5},{8,6},{9,7},{10,... | collective-permute-start | bytes 30728 | tf_op jit(solution)/shard_map/ppermute | solution.py:18
  33.3 4.8 %collective-permute-done.4 = f32[2,5,256]{2,0,1:T(2,128)S(1)} collective-permute-done((f32[2,5,256]{2,0,1:T(2,128)S(1)}, f32[2,5,256]{2,0,1:T(2,128)S(1)}, u32[]{:S(2)}, u32[]{:S(2)}) %collective-permute-start.4) | collective-permute-done | bytes 10272 | tf_op jit(solution)/shard_map/ppermute | solution.py:18
  38.2 3.2 %collective-permute-start.5 = (f32[2,5,256]{2,0,1:T(2,128)S(1)}, f32[2,5,256]{2,0,1:T(2,128)S(1)}, u32[]{:S(2)}, u32[]{:S(2)}) collective-permute-start(f32[2,5,256]{2,0,1:T(2,128)S(1)} %broadcast_select_fusion), channel_id=1, source_target_pairs={{0,60},{1,61},{2,62},{3,63},{4,0},{5,1},{6,2},{7,3},{8,4},{9,5},{1... | collective-permute-start | bytes 30728 | tf_op jit(solution)/shard_map/ppermute | solution.py:18
  41.4 4.5 %collective-permute-done.5 = f32[2,5,256]{2,0,1:T(2,128)S(1)} collective-permute-done((f32[2,5,256]{2,0,1:T(2,128)S(1)}, f32[2,5,256]{2,0,1:T(2,128)S(1)}, u32[]{:S(2)}, u32[]{:S(2)}) %collective-permute-start.5) | collective-permute-done | bytes 10272 | tf_op jit(solution)/shard_map/ppermute | solution.py:18
  45.9 11.7 %collective-permute-start.6 = (f32[2,5,256]{2,0,1:T(2,128)S(1)}, f32[2,5,256]{2,0,1:T(2,128)S(1)}, u32[]{:S(2)}, u32[]{:S(2)}) collective-permute-start(f32[2,5,256]{2,0,1:T(2,128)S(1)} %broadcast_select_fusion.1), channel_id=1, source_target_pairs={{0,56},{1,57},{2,58},{3,59},{4,60},{5,61},{6,62},{7,63},{8,0},{9,1... | collective-permute-start | bytes 30728 | tf_op jit(solution)/shard_map/ppermute | solution.py:18
  57.8 1.2 %copy-done.2 = f32[2,5,128,128]{3,1,2,0:T(8,128)S(1)} copy-done((f32[2,5,128,128]{3,1,2,0:T(8,128)S(1)}, f32[2,5,128,128]{3,1,2,0:T(8,128)}, u32[]{:S(2)}) %copy-start.2) | copy-done | bytes 655384
  58.9 1.0 slice.103
  60.3 1.1 %concatenate.19 = f32[2,5,128,128]{2,0,1,3:T(2,128)} pad(f32[2,5,128,127]{2,0,1,3:T(2,128)S(1)} %slice-done, f32[]{:T(128)} %constant.135.clone.1), padding=0_0x0_0x0_0x1_0 | pad | bytes 1305604 | tf_op jit(solution)/shard_map/concatenate | solution.py:78
  61.4 2.5 %collective-permute-done.6 = f32[2,5,256]{2,0,1:T(2,128)S(1)} collective-permute-done((f32[2,5,256]{2,0,1:T(2,128)S(1)}, f32[2,5,256]{2,0,1:T(2,128)S(1)}, u32[]{:S(2)}, u32[]{:S(2)}) %collective-permute-start.6) | collective-permute-done | bytes 10272 | tf_op jit(solution)/shard_map/ppermute | solution.py:18
  63.9 1.9 %collective-permute-start.7 = (f32[2,5,256]{2,0,1:T(2,128)S(1)}, f32[2,5,256]{2,0,1:T(2,128)S(1)}, u32[]{:S(2)}, u32[]{:S(2)}) collective-permute-start(f32[2,5,256]{2,0,1:T(2,128)S(1)} %broadcast_select_fusion.2), channel_id=1, source_target_pairs={{0,48},{1,49},{2,50},{3,51},{4,52},{5,53},{6,54},{7,55},{8,56},{9,... | collective-permute-start | bytes 30728 | tf_op jit(solution)/shard_map/ppermute | solution.py:18
  65.9 2.1 %convolution_bitcast_fusion.2 = f32[2,5,128,128]{3,1,2,0:T(8,128)} fusion(f32[2,5,1,128]{3,1,2,0:T(8,128)S(1)} %collective-permute-done.1, f32[2,5,127,128]{3,1,2,0:T(8,128)S(1)} %slice.104, f32[5,5,5]{2,1,0:T(8,128)S(1)} %copy-done.11), kind=kOutput, calls=%fused_computation.4 | convolution fusion | flops 9994240 | bytes 1708032 | tf_op jit(solution)/shard_map/uv,nuar->nvar/dot_general | solution.py:37
  67.9 4.3 %collective-permute-done.7 = f32[2,5,256]{2,0,1:T(2,128)S(1)} collective-permute-done((f32[2,5,256]{2,0,1:T(2,128)S(1)}, f32[2,5,256]{2,0,1:T(2,128)S(1)}, u32[]{:S(2)}, u32[]{:S(2)}) %collective-permute-start.7) | collective-permute-done | bytes 10272 | tf_op jit(solution)/shard_map/ppermute | solution.py:18
  72.3 3.8 %collective-permute-start.8 = (f32[2,5,256]{2,0,1:T(2,128)S(1)}, f32[2,5,256]{2,0,1:T(2,128)S(1)}, u32[]{:S(2)}, u32[]{:S(2)}) collective-permute-start(f32[2,5,256]{2,0,1:T(2,128)S(1)} %broadcast_select_fusion.3), channel_id=1, source_target_pairs={{0,32},{1,33},{2,34},{3,35},{4,36},{5,37},{6,38},{7,39},{8,40},{9,... | collective-permute-start | bytes 30728 | tf_op jit(solution)/shard_map/ppermute | solution.py:18
  77.2 1.1 copy.57
  78.3 7.3 %all-to-all-start.1 = ((f32[16,5,16,128]{3,2,1,0:T(8,128)}), f32[16,5,16,128]{3,2,1,0:T(8,128)}, u32[]{:S(2)}, u32[]{:S(2)}) async-start(f32[16,5,16,128]{3,2,1,0:T(8,128)} %copy.57), calls=%async_computation.1 | async-start | bytes 1310720 | tf_op jit(solution)/shard_map/all_to_all | solution.py:90
  86.7 1.5 %copy.51 = f32[2,5,128,128]{3,1,2,0:T(8,128)S(1)} copy(f32[2,5,128,128]{2,0,1,3:T(2,128)} %fusion.37) | data formatting | bytes 1310720 | tf_op jit(solution)/shard_map/scatter-add | solution.py:80
  88.2 1.0 convolution_bitcast_fusion.1
  89.7 1.1 %fusion.4 = f32[2,5,128,128]{3,1,2,0:T(8,128)S(1)} fusion(f32[2,5,128,128]{3,1,2,0:T(8,128)S(1)} %convolution_bitcast_fusion.1, f32[2,5,128,128]{3,1,2,0:T(8,128)S(1)} %copy-done.5, f32[2,5,128,128]{3,1,2,0:T(8,128)S(1)} %fusion.5, f32[2,5,127,128]{3,1,2,0:T(8,128)S(1)} %copy-done.6, f32[2,5,1,128]{3,1,2,0:T(8,128)S(1)} %collective-permute-done, ...), kind=kOutput, calls=%fused_computation.8 | convolution fusion | flops 10485760 | bytes 4853760 | tf_op jit(solution)/shard_map/uv,nuar->nvar/dot_general | solution.py:37
  90.8 10.8 %all-to-all-done.1 = f32[16,5,16,128]{3,2,1,0:T(8,128)} async-done(((f32[16,5,16,128]{3,2,1,0:T(8,128)}), f32[16,5,16,128]{3,2,1,0:T(8,128)}, u32[]{:S(2)}, u32[]{:S(2)}) %all-to-all-start.1) | async-done | bytes 655392 | tf_op jit(solution)/shard_map/all_to_all | solution.py:90
  101.6 1.3 %copy.58 = f32[8,2,5,16,128]{4,2,3,0,1:T(8,128)S(1)} copy(f32[8,2,5,16,128]{4,3,2,1,0:T(8,128)} %bitcast.29) | data formatting | bytes 1310720 | tf_op jit(solution)/shard_map/all_to_all | solution.py:90
  102.9 1.2 %fusion.1 = f32[2,5,128,128]{3,1,2,0:T(8,128)S(1)} fusion(f32[2,5,128,128]{3,1,2,0:T(8,128)S(1)} %fusion.4, f32[2,5,128,128]{3,1,2,0:T(8,128)S(1)} %bitcast.83, f32[2,5,128,127]{3,1,2,0:T(8,128)S(1)} %slice_multiply_fusion, f32[128,128]{1,0:T(8,128)S(1)} %broadcast_multiply_fusion.4, f32[5,5,5]{2,1,0:T(8,128)S(1)} %copy-done.11), kind=kOutput, calls=%fused_computation.2 | convolution fusion | flops 10321920 | bytes 3870720 | tf_op jit(solution)/shard_map/uv,nuar->nvar/dot_general | solution.py:37
  104.1 1.0 copy.59
  (60 shorter events, 6.4 us)
Async XLA Ops:
  0.0 1.2 %copy-start = (f32[2,5,128,128]{3,2,1,0:T(8,128)S(1)}, f32[2,5,128,128]{3,2,1,0:T(8,128)}, u32[]{:S(2)}) copy-start(f32[2,5,128,128]{3,2,1,0:T(8,128)} %param.8) | copy-start | bytes 1966084
  2.4 2.0 %copy-start.7 = (f32[2,5,128,128]{2,0,1,3:T(2,128)}, f32[2,5,128,128]{2,0,1,3:T(2,128)S(1)}, u32[]{:S(2)}) copy-start(f32[2,5,128,128]{2,0,1,3:T(2,128)S(1)} %broadcast_multiply_fusion.2) | copy-start | bytes 1966084
  2.4 22.1 %collective-permute-start.2 = (f32[2,5,128]{2,0,1:T(2,128)S(1)}, f32[2,5,128]{2,0,1:T(2,128)S(1)}, u32[]{:S(2)}, u32[]{:S(2)}) collective-permute-start(f32[2,5,128]{2,0,1:T(2,128)S(1)} %slice_bitcast_fusion.5), channel_id=1, source_target_pairs={{0,1},{1,0},{2,3},{3,2},{4,5},{5,4},{6,7},{7,6},{8,9},{9,8},{10,11... | collective-permute-start | bytes 15368 | tf_op jit(solution)/shard_map/ppermute | solution.py:24
  4.8 2.0 %copy-start.1 = (f32[2,5,128,128]{3,1,2,0:T(8,128)}, f32[2,5,128,128]{3,1,2,0:T(8,128)S(1)}, u32[]{:S(2)}) copy-start(f32[2,5,128,128]{3,1,2,0:T(8,128)S(1)} %get-tuple-element.22) | copy-start | bytes 1966084
  4.8 2.0 %copy-start.3 = (f32[2,5,128,128]{3,1,2,0:T(8,128)}, f32[2,5,128,128]{3,1,2,0:T(8,128)S(1)}, u32[]{:S(2)}) copy-start(f32[2,5,128,128]{3,1,2,0:T(8,128)S(1)} %get-tuple-element.23) | copy-start | bytes 1966084
  4.8 61.0 %collective-permute-start.1 = (f32[2,5,1,128]{3,1,2,0:T(8,128)S(1)}, f32[2,5,1,128]{3,1,2,0:T(8,128)S(1)}, u32[]{:S(2)}, u32[]{:S(2)}) collective-permute-start(f32[2,5,1,128]{3,1,2,0:T(8,128)S(1)} %slice.105), channel_id=1, source_target_pairs={{0,62},{1,63},{2,0},{3,1},{4,2},{5,3},{6,4},{7,5},{8,6},{9,7},{10,... | collective-permute-start | bytes 15368 | tf_op jit(solution)/shard_map/ppermute | solution.py:18
  6.8 82.4 %collective-permute-start = (f32[2,5,1,128]{3,1,2,0:T(8,128)S(1)}, f32[2,5,1,128]{3,1,2,0:T(8,128)S(1)}, u32[]{:S(2)}, u32[]{:S(2)}) collective-permute-start(f32[2,5,1,128]{3,1,2,0:T(8,128)S(1)} %slice.102), channel_id=1, source_target_pairs={{0,2},{1,3},{2,4},{3,5},{4,6},{5,7},{6,8},{7,9},{8,10},{9,11},{10,... | collective-permute-start | bytes 15368 | tf_op jit(solution)/shard_map/ppermute | solution.py:18
  13.6 62.5 %all-to-all-start = ((f32[2,5,128,128]{3,1,0,2:T(8,128)}), f32[2,5,128,128]{3,1,0,2:T(8,128)S(1)}, u32[]{:S(2)}, u32[]{:S(2)}) async-start(f32[2,5,128,128]{3,1,0,2:T(8,128)} %copy.55), calls=%async_computation | async-start | bytes 2097152 | tf_op jit(solution)/shard_map/all_to_all | solution.py:87
  20.8 0.7 copy-start.12
  21.7 1.1 %copy-start.9 = (f32[2,5,128,128]{3,2,1,0:T(8,128)S(1)}, f32[2,5,128,128]{3,2,1,0:T(8,128)}, u32[]{:S(2)}) copy-start(f32[2,5,128,128]{3,2,1,0:T(8,128)} %param.9) | copy-start | bytes 1966084
  21.7 1.1 %copy-start.11 = (f32[5,5,5]{2,1,0:T(8,128)S(1)}, f32[5,5,5]{2,1,0:T(8,128)}, u32[]{:S(2)}) copy-start(f32[5,5,5]{2,1,0:T(8,128)} %param.12) | copy-start | bytes 1504
  22.8 18.6 %copy-start.10 = (f32[128,128]{1,0:T(8,128)S(1)}, f32[128,128]{1,0:T(8,128)}, u32[]{:S(2)}) copy-start(f32[128,128]{1,0:T(8,128)} %param.11) | copy-start | bytes 196612
  24.4 33.3 %copy-start.4 = (f32[2,5,128,128]{3,1,2,0:T(8,128)S(1)}, f32[2,5,128,128]{3,1,2,0:T(8,128)}, u32[]{:S(2)}) copy-start(f32[2,5,128,128]{3,1,2,0:T(8,128)} %copy-done.3) | copy-start | bytes 1966084
  24.5 6.9 %collective-permute-start.3 = (f32[2,5,128]{2,0,1:T(2,128)S(1)}, f32[2,5,128]{2,0,1:T(2,128)S(1)}, u32[]{:S(2)}, u32[]{:S(2)}) collective-permute-start(f32[2,5,128]{2,0,1:T(2,128)S(1)} %collective-permute-done.2), channel_id=1, source_target_pairs={{0,62},{1,63},{2,0},{3,1},{4,2},{5,3},{6,4},{7,5},{8,6},{9,7},{10,... | collective-permute-start | bytes 15368 | tf_op jit(solution)/shard_map/ppermute | solution.py:18
  31.3 6.8 %collective-permute-start.4 = (f32[2,5,256]{2,0,1:T(2,128)S(1)}, f32[2,5,256]{2,0,1:T(2,128)S(1)}, u32[]{:S(2)}, u32[]{:S(2)}) collective-permute-start(f32[2,5,256]{2,0,1:T(2,128)S(1)} %constant_dynamic-update-slice_fusion), channel_id=1, source_target_pairs={{0,62},{1,63},{2,0},{3,1},{4,2},{5,3},{6,4},{7,5},{8,6},{9,7},{10,... | collective-permute-start | bytes 30728 | tf_op jit(solution)/shard_map/ppermute | solution.py:18
  38.2 7.7 %collective-permute-start.5 = (f32[2,5,256]{2,0,1:T(2,128)S(1)}, f32[2,5,256]{2,0,1:T(2,128)S(1)}, u32[]{:S(2)}, u32[]{:S(2)}) collective-permute-start(f32[2,5,256]{2,0,1:T(2,128)S(1)} %broadcast_select_fusion), channel_id=1, source_target_pairs={{0,60},{1,61},{2,62},{3,63},{4,0},{5,1},{6,2},{7,3},{8,4},{9,5},{1... | collective-permute-start | bytes 30728 | tf_op jit(solution)/shard_map/ppermute | solution.py:18
  45.9 17.9 %collective-permute-start.6 = (f32[2,5,256]{2,0,1:T(2,128)S(1)}, f32[2,5,256]{2,0,1:T(2,128)S(1)}, u32[]{:S(2)}, u32[]{:S(2)}) collective-permute-start(f32[2,5,256]{2,0,1:T(2,128)S(1)} %broadcast_select_fusion.1), channel_id=1, source_target_pairs={{0,56},{1,57},{2,58},{3,59},{4,60},{5,61},{6,62},{7,63},{8,0},{9,1... | collective-permute-start | bytes 30728 | tf_op jit(solution)/shard_map/ppermute | solution.py:18
  57.7 1.2 %copy-start.2 = (f32[2,5,128,128]{3,1,2,0:T(8,128)S(1)}, f32[2,5,128,128]{3,1,2,0:T(8,128)}, u32[]{:S(2)}) copy-start(f32[2,5,128,128]{3,1,2,0:T(8,128)} %copy-done.1) | copy-start | bytes 1966084
  58.9 1.3 %slice-start = ((f32[2,5,128,128]{2,0,1,3:T(2,128)}), f32[2,5,128,127]{2,0,1,3:T(2,128)S(1)}, s32[]{:S(2)}) async-start(f32[2,5,128,128]{2,0,1,3:T(2,128)} %copy-done.7), calls=%async_computation.2 | async-start | bytes 1300480 | tf_op jit(solution)/shard_map/slice | solution.py:78
  63.9 8.3 %collective-permute-start.7 = (f32[2,5,256]{2,0,1:T(2,128)S(1)}, f32[2,5,256]{2,0,1:T(2,128)S(1)}, u32[]{:S(2)}, u32[]{:S(2)}) collective-permute-start(f32[2,5,256]{2,0,1:T(2,128)S(1)} %broadcast_select_fusion.2), channel_id=1, source_target_pairs={{0,48},{1,49},{2,50},{3,51},{4,52},{5,53},{6,54},{7,55},{8,56},{9,... | collective-permute-start | bytes 30728 | tf_op jit(solution)/shard_map/ppermute | solution.py:18
  72.3 13.3 %collective-permute-start.8 = (f32[2,5,256]{2,0,1:T(2,128)S(1)}, f32[2,5,256]{2,0,1:T(2,128)S(1)}, u32[]{:S(2)}, u32[]{:S(2)}) collective-permute-start(f32[2,5,256]{2,0,1:T(2,128)S(1)} %broadcast_select_fusion.3), channel_id=1, source_target_pairs={{0,32},{1,33},{2,34},{3,35},{4,36},{5,37},{6,38},{7,39},{8,40},{9,... | collective-permute-start | bytes 30728 | tf_op jit(solution)/shard_map/ppermute | solution.py:18
  78.3 7.8 %copy-start.8 = (f32[2,5,128,128]{2,0,1,3:T(2,128)S(1)}, f32[2,5,128,128]{2,0,1,3:T(2,128)}, u32[]{:S(2)}) copy-start(f32[2,5,128,128]{2,0,1,3:T(2,128)} %copy-done.7) | copy-start | bytes 1966084
  78.3 23.3 %all-to-all-start.1 = ((f32[16,5,16,128]{3,2,1,0:T(8,128)}), f32[16,5,16,128]{3,2,1,0:T(8,128)}, u32[]{:S(2)}, u32[]{:S(2)}) async-start(f32[16,5,16,128]{3,2,1,0:T(8,128)} %copy.57), calls=%async_computation.1 | async-start | bytes 1310720 | tf_op jit(solution)/shard_map/all_to_all | solution.py:90
  88.1 1.2 %copy-start.5 = (f32[2,5,128,128]{3,1,2,0:T(8,128)S(1)}, f32[2,5,128,128]{3,1,2,0:T(8,128)}, u32[]{:S(2)}) copy-start(f32[2,5,128,128]{3,1,2,0:T(8,128)} %convolution_bitcast_fusion.2) | copy-start | bytes 1966084
  88.2 1.5 %copy-start.6 = (f32[2,5,127,128]{3,1,2,0:T(8,128)S(1)}, f32[2,5,127,128]{3,1,2,0:T(8,128)}, u32[]{:S(2)}) copy-start(f32[2,5,127,128]{3,1,2,0:T(8,128)} %slice.103) | copy-start | bytes 1950724
where the time goes:
time: 106 us; the launch traced here: 105 us
  starting transfers between devices  48.3 us (46%)
  waiting for transfers between devices  31.7 us (30%)
  local copies, waits for them, and re-layouts  14.3 us (13%)
  matrix products  8.01 us (8%)
  other arithmetic  2.47 us (2%)
    ppermute x8, starting transfers between devices, from_behind(): return lax.ppermute(value, axis, pairs)  32 us
    ppermute x8, waiting for transfers between devices, from_behind(): return lax.ppermute(value, axis, pairs)  20.9 us
    all_to_all x1, waiting for transfers between devices, local(): lax.all_to_all(turned, 'inst', split_axis=0, concat_axis=2, tiled=True)  10.8 us
    all_to_all x1, starting transfers between devices, local(): lax.all_to_all(turned, 'inst', split_axis=0, concat_axis=2, tiled=True)  7.34 us
    all_to_all x1, starting transfers between devices, local(): lax.all_to_all(adjoint, 'inst', split_axis=2, concat_axis=0, tiled=True)  7.1 us
    dot_general x5, matrix products, mix(): return jnp.einsum('uv,nuar->nvar', matrix, grid_field, precision=highest)  7.09 us
    unnamed x29, local copies, waits for them, and re-layouts  5.21 us
  transfers between devices with their start and end apart: 11, of which 6 were waited for; matrix products, arithmetic and copies ran while one was open for 15% of the time, Pallas kernels for 0%

commit v1 on v0

v1 whole, which is shorter than its diff:
```python
import functools

import numpy as np

import jax
import jax.numpy as jnp
from jax import lax
from jax.experimental import pallas as pl
from jax.experimental.pallas import tpu as pltpu
from jax.sharding import PartitionSpec as P

MESH = pl.DeviceIdType.MESH
NI = 16
ND = 8
NV = 5
NB = 4
FB = 32
BLK = 16
ROWS = 128
LANES = 128
SPIN_RATE = 0.75
CHUNKS = ((0, 3), (3, 2))
ORDER = (4, 3, 5, 2, 6, 1, 7)
VMEM_LIMIT = 48 * 1024 * 1024


def spectral_entries():
    offset = np.arange(1, NI)
    angle = np.pi * offset / NI
    entries = 0.5 * np.where(offset % 2 == 0, 1.0, -1.0) * np.cos(angle) / np.sin(angle)
    return np.concatenate([[0.0], entries])


def payload_kernel(adj, coef, out):
    lane = lax.broadcasted_iota(jnp.int32, (ROWS, LANES), 1)
    faces = jnp.zeros((ROWS, LANES), jnp.float32)
    outward = coef[3]
    for k in range(2 * NV):
        n, u = divmod(k, NV)
        moved = pltpu.roll(outward * adj[n, u], k + 1, 1)
        faces = jnp.where(lane == k, moved, faces)
    out[0:16, :] = faces.T[0:16, :]
    for k in range(2 * NV):
        n, u = divmod(k, NV)
        out[10 + k : 11 + k, :] = coef[1, ROWS - 1 : ROWS, :] * adj[n, u, ROWS - 1 : ROWS, :]
        out[20 + k : 21 + k, :] = coef[2, 0:1, :] * adj[n, u, 0:1, :]
    out[30:32, :] = jnp.zeros((2, LANES), jnp.float32)


def main_kernel(
    adj_hbm, src_hbm, coef_hbm, vol_hbm, mixing, _, out_hbm,
    adj, base, coef, vol, ahead, behind, gathered, turned, spectral,
    load_sem, store_sem, send1, recv1, send2, recv2,
):
    me = lax.axis_index("inst")
    barrier = pltpu.get_barrier_semaphore()
    for d in range(1, ND):
        pl.semaphore_signal(barrier, inc=1, device_id={"inst": lax.rem(me + d, ND)}, device_id_type=MESH)
    loads = [
        pltpu.make_async_copy(s, t, load_sem.at[i])
        for i, (s, t) in enumerate(((adj_hbm, adj), (coef_hbm, coef), (src_hbm, base), (vol_hbm, vol)))
    ]
    for copy in loads:
        copy.start()
    pl.semaphore_wait(barrier, ND - 1)

    my_rows = pl.ds(pl.multiple_of(me * BLK, BLK), BLK)

    def first(c, d):
        v0, nv = CHUNKS[c]
        to = lax.rem(me + d, ND)
        return pltpu.make_async_remote_copy(
            src_ref=adj_hbm.at[:, pl.ds(v0, nv), pl.ds(pl.multiple_of(to * BLK, BLK), BLK)],
            dst_ref=gathered.at[d, :, pl.ds(v0, nv)],
            send_sem=send1.at[c, d], recv_sem=recv1.at[c, d],
            device_id={"inst": to}, device_id_type=MESH,
        )

    def second(c, d):
        v0, nv = CHUNKS[c]
        to = lax.rem(me + d, ND)
        return pltpu.make_async_remote_copy(
            src_ref=turned.at[d, :, pl.ds(v0, nv)],
            dst_ref=spectral.at[:, pl.ds(v0, nv), my_rows],
            send_sem=send2.at[c, d], recv_sem=recv2.at[c, d],
            device_id={"inst": to}, device_id_type=MESH,
        )

    chunks = range(len(CHUNKS))
    for c in chunks:
        for d in ORDER:
            first(c, d).start()
    for copy in loads:
        copy.wait()

    lane = lax.broadcasted_iota(jnp.int32, (BLK, LANES), 1)

    def stencil(step, carry):
        n = step // (ROWS // BLK)
        rows = pl.ds(pl.multiple_of(lax.rem(step, ROWS // BLK) * BLK, BLK), BLK)
        field = [adj[n, u, rows, :] for u in range(NV)]
        total = [base[n, v, rows, :] for v in range(NV)]
        for k in range(5):
            scale = coef[k, rows, :]
            q = [scale * f for f in field]
            for v in range(NV):
                mixed = mixing[k, 0, v] * q[0]
                for u in range(1, NV):
                    mixed = mixed + mixing[k, u, v] * q[u]
                if k == 0:
                    total[v] = total[v] + mixed
                elif k == 1:
                    ahead[n, v, rows, :] = mixed
                elif k == 2:
                    behind[n, v, rows, :] = mixed
                elif k == 3:
                    total[v] = total[v] + jnp.where(lane == 0, 0.0, pltpu.roll(mixed, 1, 1))
                else:
                    total[v] = total[v] + jnp.where(lane == LANES - 1, 0.0, pltpu.roll(mixed, LANES - 1, 1))
        for v in range(NV):
            base[n, v, rows, :] = total[v]
        return carry

    lax.fori_loop(0, 2 * (ROWS // BLK), stencil, 0)

    row = lax.broadcasted_iota(jnp.int32, (ROWS, LANES), 0)

    def moved(step, carry):
        n, v = step // NV, lax.rem(step, NV)
        down = jnp.where(row == 0, 0.0, pltpu.roll(ahead[n, v], 1, 0))
        up = jnp.where(row == ROWS - 1, 0.0, pltpu.roll(behind[n, v], ROWS - 1, 0))
        base[n, v] = base[n, v] + (down + up)
        return carry

    lax.fori_loop(0, 2 * NV, moved, 0)

    entries = spectral_entries()
    half = NI // 2

    def transform(c):
        v0, nv = CHUNKS[c]

        def body(step, carry):
            v = v0 + step // 2
            part = lax.rem(step, 2) * 8
            rows = pl.ds(pl.multiple_of(part, 8), 8)
            mine = pl.ds(pl.multiple_of(me * BLK + part, 8), 8)
            x = []
            for a in range(NI):
                slot, i = (-(a // 2)) % ND, a % 2
                x.append(adj[i, v, mine, :] if slot == 0 else gathered[slot, i, v, rows, :])
            plus = [x[a] + x[a + half] for a in range(half)]
            minus = [x[a] - x[a + half] for a in range(half)]
            for b in range(half):
                even, odd = None, None
                for a in range(half):
                    low, high = entries[(a - b) % NI], entries[(a + half - b) % NI]
                    even_term = np.float32(0.5 * (low + high)) * plus[a]
                    odd_term = np.float32(0.5 * (low - high)) * minus[a]
                    even = even_term if even is None else even + even_term
                    odd = odd_term if odd is None else odd + odd_term
                for n, value in ((b, even + odd), (b + half, even - odd)):
                    slot, j = n // 2, n % 2
                    if slot == 0:
                        spectral[j, v, mine, :] = value
                    else:
                        turned[slot, j, v, rows, :] = value
            return carry

        lax.fori_loop(0, 2 * nv, body, 0)

    for c in chunks:
        for d in ORDER:
            first(c, d).wait_recv()
        transform(c)
        for d in ORDER:
            second(c, d).start()

    stores = []
    for c in chunks:
        v0, nv = CHUNKS[c]
        for d in ORDER:
            second(c, d).wait_recv()

        def finish(step, carry, v0=v0):
            v = v0 + step // 2
            n = lax.rem(step, 2)
            base[n, v] = base[n, v] + (SPIN_RATE * vol[...]) * spectral[n, v]
            return carry

        lax.fori_loop(0, 2 * nv, finish, 0)
        store = pltpu.make_async_copy(
            base.at[:, pl.ds(v0, nv)], out_hbm.at[:, pl.ds(v0, nv)], store_sem.at[c]
        )
        store.start()
        stores.append(store)
    for c in chunks:
        for d in ORDER:
            first(c, d).wait_send()
            second(c, d).wait_send()
    for store in stores:
        store.wait()


def last_kernel(part, received, mixing, partner, out, halo, face, sems):
    p = lax.axis_index("space")
    count = 64
    copies = [
        pltpu.make_async_copy(received.at[lax.rem(p + count - 2, count)], halo.at[0], sems.at[8]),
        pltpu.make_async_copy(received.at[lax.rem(p + 2, count)], halo.at[1], sems.at[9]),
    ]
    shifts = []
    for n in range(2):
        for b in range(NB):
            x = partner[n, NB * p + b]
            shifts.append(lax.rem(b - lax.rem(x, NB) + NB, NB) * FB)
            copies.append(
                pltpu.make_async_copy(received.at[x // NB, pl.ds(0, 16)], face.at[n * NB + b], sems.at[n * NB + b])
            )
    for copy in copies:
        copy.start()
    for copy in copies:
        copy.wait()
    lane = lax.broadcasted_iota(jnp.int32, (16, LANES), 1)
    mixed = []
    for n in range(2):
        rows = jnp.zeros((16, LANES), jnp.float32)
        for b in range(NB):
            rows = jnp.where(lane // FB == b, pltpu.roll(face[n * NB + b], shifts[n * NB + b], 1), rows)
        for v in range(NV):
            mixed.append(sum(mixing[3, u, v] * rows[n * NV + u : n * NV + u + 1, :] for u in range(NV)))
    mixed = jnp.concatenate(mixed + [jnp.zeros((LANES - 2 * NV, LANES), jnp.float32)], axis=0).T
    wide = lax.broadcasted_iota(jnp.int32, (ROWS, LANES), 1)
    for k in range(2 * NV):
        n, v = divmod(k, NV)
        column = pltpu.roll(mixed, LANES - 1 - k, 1)
        out[n, v] = part[n, v] + jnp.where(wide == LANES - 1, column, 0.0)
        first = sum(mixing[1, u, v] * halo[0, 10 + n * NV + u : 11 + n * NV + u, :] for u in range(NV))
        last = sum(mixing[2, u, v] * halo[1, 20 + n * NV + u : 21 + n * NV + u, :] for u in range(NV))
        out[n, v, 0:1, :] = out[n, v, 0:1, :] + first
        out[n, v, ROWS - 1 : ROWS, :] = out[n, v, ROWS - 1 : ROWS, :] + last


def local(adjoint, source, coefficient, volume, mixing, face_partner):
    f32 = jnp.float32
    vmem, smem, anywhere = (pl.BlockSpec(memory_space=s) for s in (pltpu.VMEM, pltpu.SMEM, pl.ANY))
    payload = pl.pallas_call(
        payload_kernel,
        out_shape=jax.ShapeDtypeStruct((32, LANES), f32),
        in_specs=[vmem, vmem],
        out_specs=vmem,
        name="payload",
    )(adjoint, coefficient)
    received = lax.all_gather(payload, "space")
    shard = (2, NV, ROWS, LANES)
    nc = len(CHUNKS)
    part = pl.pallas_call(
        main_kernel,
        out_shape=jax.ShapeDtypeStruct(shard, f32),
        in_specs=[anywhere, anywhere, anywhere, anywhere, smem, anywhere],
        out_specs=anywhere,
        scratch_shapes=[
            pltpu.VMEM(shard, f32), pltpu.VMEM(shard, f32),
            pltpu.VMEM((5, ROWS, LANES), f32), pltpu.VMEM((ROWS, LANES), f32),
            pltpu.VMEM(shard, f32), pltpu.VMEM(shard, f32),
            pltpu.VMEM((ND, 2, NV, BLK, LANES), f32), pltpu.VMEM((ND, 2, NV, BLK, LANES), f32),
            pltpu.VMEM(shard, f32),
            pltpu.SemaphoreType.DMA((4,)), pltpu.SemaphoreType.DMA((nc,)),
            pltpu.SemaphoreType.DMA((nc, ND)), pltpu.SemaphoreType.DMA((nc, ND)),
            pltpu.SemaphoreType.DMA((nc, ND)), pltpu.SemaphoreType.DMA((nc, ND)),
        ],
        compiler_params=pltpu.CompilerParams(
            collective_id=0, has_side_effects=True, vmem_limit_bytes=VMEM_LIMIT
        ),
        cost_estimate=pl.CostEstimate(flops=20_000_000, bytes_accessed=60_000_000, transcendentals=0),
        name="spectral_and_stencil",
    )(adjoint, source, coefficient, volume, mixing, payload)
    return pl.pallas_call(
        last_kernel,
        out_shape=jax.ShapeDtypeStruct(shard, f32),
        in_specs=[vmem, anywhere, smem, smem],
        out_specs=vmem,
        scratch_shapes=[
            pltpu.VMEM((2, 32, LANES), f32), pltpu.VMEM((2 * NB, 16, LANES), f32),
            pltpu.SemaphoreType.DMA((10,)),
        ],
        name="boundaries",
    )(part, received, mixing, face_partner)


def solution(mesh):
    in_specs = (
        P("inst", None, "space", None),
        P("inst", None, "space", None),
        P(None, "space", None),
        P("space", None),
        P(),
        P("inst", None),
    )
    out_specs = P("inst", None, "space", None)
    return jax.shard_map(local, mesh=mesh, in_specs=in_specs, out_specs=out_specs, check_vma=False)
```

time: 106 us -> 110 us (1.038)
  the two profiles are of different devices: /device:TPU:198 before, /device:TPU:1 now
where the time goes in v1:
time: 110 us; the launch traced here: 109 us
  waiting for transfers between devices  48.9 us (44%)
  Pallas kernels  42.9 us (39%)
  between operations  13.4 us (12%)
  local copies, waits for them, and re-layouts  4.2 us (4%)
    all_gather x1, waiting for transfers between devices, local(): received = lax.all_gather(payload, 'space')  48.9 us
    pallas_call x1, Pallas kernels, local(): pl.pallas_call(main_kernel, out_shape=jax.ShapeDtypeStruct(shard, f32), i...  37.3 us
    unnamed x14, local copies, waits for them, and re-layouts  4.2 us
    pallas_call x1, Pallas kernels, local(): pl.pallas_call(last_kernel, out_shape=jax.ShapeDtypeStruct(shard, f32), i...  3.41 us
  transfers between devices with their start and end apart: 1, of which 1 were waited for; matrix products, arithmetic and copies ran while one was open for 0% of the time, Pallas kernels for 34%

profile of v1, /device:TPU:1, one launch (start us, length us, event | category | flops | bytes accessed | tf_op | source)
XLA Modules:
  0.0 109.4 jit_solution(8784791263115918455)
XLA Ops:
  6.5 0.0 copy-start.2
  6.5 0.0 copy-start
  6.5 0.0 all-gather.3.cloned.1.call-start
  6.5 2.1 %payload.1._ = f32[32,128]{1,0:T(8,128)} custom-call(f32[2,5,128,128]{3,2,1,0:T(8,128)} %adj_hbm.1, f32[5,128,128]{2,1,0:T(8,128)} %coef_hbm.1), custom_call_target="tpu_custom_call" | custom-call | tf_op jit(solution)/shard_map/payload/pallas_call | solution.py:247
  8.7 0.0 copy-start.4
  8.7 0.0 all-gather.3.cloned.1.call-update
  8.7 0.0 copy-done.2
  8.7 0.0 copy-done
  8.7 0.7 copy-done.4
  9.4 0.0 copy-start.3
  9.4 1.1 copy-done.3
  10.5 0.0 copy-start.5
  10.5 0.7 copy-done.5
  11.2 0.0 copy-start.6
  11.2 0.8 copy-done.6
  12.1 37.3 %spectral_and_stencil.1.part = f32[2,5,128,128]{3,2,1,0:T(8,128)S(1)} custom-call(f32[2,5,128,128]{3,2,1,0:T(8,128)S(1)} %copy-done, f32[2,5,128,128]{3,2,1,0:T(8,128)S(1)} %copy-done.3, f32[5,128,128]{2,1,0:T(8,128)S(1)} %copy-done.2, f32[128,128]{1,0:T(8,128)S(1)} %copy-done.6, f32[5,5,5]{2,1,0:T(8,128)S(1)} %copy-done.5, f32[32,128]{1,0:T(8,128)S(1)} %copy-done.4), custom_call_target="tpu_custom_call" | custom-call | flops 20000000 | bytes 60000000 | tf_op jit(solution)/shard_map/spectral_and_stencil/pallas_call | solution.py:257
  49.4 0.0 copy-start.1
  49.4 0.9 copy-done.1
  50.2 48.9 %all-gather.3.cloned.1.call-done = f32[2048,128]{1,0:T(8,128)} async-done(((f32[32,128]{1,0:T(8,128)}), f32[2048,128]{1,0:T(8,128)}) %all-gather.3.cloned.1.call-update) | async-done | bytes 1048592 | tf_op jit(solution)/shard_map/all_gather | solution.py:254
  99.2 3.4 %boundaries.1 = f32[2,5,128,128]{3,2,1,0:T(8,128)} custom-call(f32[2,5,128,128]{3,2,1,0:T(8,128)} %copy-done.1, f32[64,32,128]{2,1,0:T(8,128)} %bitcast.1, f32[5,5,5]{2,1,0:T(8,128)} %mixing.3, s32[2,256]{1,0:T(2,128)} %partner.1), custom_call_target="tpu_custom_call" | custom-call | tf_op jit(solution)/shard_map/boundaries/pallas_call | solution.py:278
Async XLA Ops:
  6.5 2.2 %copy-start.2 = (f32[5,128,128]{2,1,0:T(8,128)S(1)}, f32[5,128,128]{2,1,0:T(8,128)}, u32[]{:S(2)}) copy-start(f32[5,128,128]{2,1,0:T(8,128)} %coef_hbm.1) | copy-start | bytes 983044
  6.5 2.2 %copy-start = (f32[2,5,128,128]{3,2,1,0:T(8,128)S(1)}, f32[2,5,128,128]{3,2,1,0:T(8,128)}, u32[]{:S(2)}) copy-start(f32[2,5,128,128]{3,2,1,0:T(8,128)} %adj_hbm.1) | copy-start | bytes 1966084
  6.5 92.6 %all-gather.3.cloned.1.call-start = ((), (), s32[]{:S(2)}) async-start(), calls=%async_computation | async-start | bytes 1064960 | tf_op jit(solution)/shard_map/all_gather | solution.py:254
  8.7 0.7 copy-start.4
  9.4 1.1 copy-start.3
  10.5 0.7 copy-start.5
  11.2 0.8 copy-start.6
  49.4 0.9 copy-start.1
Sparse Core Ops, SparseCore 0:
  10.7 88.3 all-gather.2

commit v2 on v1

--- a/solution.py
+++ b/solution.py
@@ -12,6 +12,10 @@
 MESH = pl.DeviceIdType.MESH
 NI = 16
 ND = 8
+NX = 4
+NZ = 8
+SECTORS = NX * NZ
+SPACE = 2 * SECTORS
 NV = 5
 NB = 4
 FB = 32
@@ -21,7 +25,7 @@
 SPIN_RATE = 0.75
 CHUNKS = ((0, 3), (3, 2))
 ORDER = (4, 3, 5, 2, 6, 1, 7)
-VMEM_LIMIT = 48 * 1024 * 1024
+VMEM_LIMIT = 56 * 1024 * 1024
 
 
 def spectral_entries():
@@ -31,38 +35,46 @@
     return np.concatenate([[0.0], entries])
 
 
-def payload_kernel(adj, coef, out):
-    lane = lax.broadcasted_iota(jnp.int32, (ROWS, LANES), 1)
-    faces = jnp.zeros((ROWS, LANES), jnp.float32)
-    outward = coef[3]
-    for k in range(2 * NV):
-        n, u = divmod(k, NV)
-        moved = pltpu.roll(outward * adj[n, u], k + 1, 1)
-        faces = jnp.where(lane == k, moved, faces)
-    out[0:16, :] = faces.T[0:16, :]
-    for k in range(2 * NV):
-        n, u = divmod(k, NV)
-        out[10 + k : 11 + k, :] = coef[1, ROWS - 1 : ROWS, :] * adj[n, u, ROWS - 1 : ROWS, :]
-        out[20 + k : 21 + k, :] = coef[2, 0:1, :] * adj[n, u, 0:1, :]
-    out[30:32, :] = jnp.zeros((2, LANES), jnp.float32)
-
-
 def main_kernel(
-    adj_hbm, src_hbm, coef_hbm, vol_hbm, mixing, _, out_hbm,
-    adj, base, coef, vol, ahead, behind, gathered, turned, spectral,
-    load_sem, store_sem, send1, recv1, send2, recv2,
+    adj_hbm, src_hbm, coef_hbm, vol_hbm, mixing, partner, out_hbm,
+    adj, base, coef, vol, ahead, behind, gathered, turned, spectral, payload, faces, edges, halos,
+    load_sem, store_sem, send1, recv1, send2, recv2, face_send, face_recv, halo_send, halo_recv,
 ):
     me = lax.axis_index("inst")
+    p = lax.axis_index("space")
+    side = lax.rem(p, 2)
+    z, x = lax.rem(p // 2, NZ), p // (2 * NZ)
+    rank = z * NX + x
+    earlier = rank + 1 - side
+    next_earlier, prev_earlier = z == NZ - 1, z != 0
+    next_id = {"space": lax.rem(p + 2, SPACE)}
+    prev_id = {"space": lax.rem(p + SPACE - 2, SPACE)}
+
+    def across(r):
+        return {"space": 2 * (lax.rem(r, NX) * NZ + r // NX) + 1 - side}
+
     barrier = pltpu.get_barrier_semaphore()
+
+    def greet(device):
+        pl.semaphore_signal(barrier, inc=1, device_id=device, device_id_type=MESH)
+
     for d in range(1, ND):
-        pl.semaphore_signal(barrier, inc=1, device_id={"inst": lax.rem(me + d, ND)}, device_id_type=MESH)
+        greet({"inst": lax.rem(me + d, ND)})
+
+    def greet_across(r, carry):
+        greet(across(r))
+        return carry
+
+    lax.fori_loop(earlier, SECTORS, greet_across, 0)
+    pl.when(jnp.logical_not(next_earlier))(lambda: greet(next_id))
+    pl.when(jnp.logical_not(prev_earlier))(lambda: greet(prev_id))
     loads = [
         pltpu.make_async_copy(s, t, load_sem.at[i])
         for i, (s, t) in enumerate(((adj_hbm, adj), (coef_hbm, coef), (src_hbm, base), (vol_hbm, vol)))
     ]
     for copy in loads:
         copy.start()
-    pl.semaphore_wait(barrier, ND - 1)
+    pl.semaphore_wait(barrier, ND - 1 + earlier + next_earlier.astype(jnp.int32) + prev_earlier.astype(jnp.int32))
 
     my_rows = pl.ds(pl.multiple_of(me * BLK, BLK), BLK)
 
@@ -86,12 +98,53 @@
             device_id={"inst": to}, device_id_type=MESH,
         )
 
+    def face_to(r):
+        return pltpu.make_async_remote_copy(
+            src_ref=payload, dst_ref=faces.at[rank],
+            send_sem=face_send.at[r], recv_sem=face_recv.at[rank],
+            device_id=across(r), device_id_type=MESH,
+        )
+
+    def face_from(r):
+        return pltpu.make_async_remote_copy(
+            src_ref=payload, dst_ref=faces.at[r],
+            send_sem=face_send.at[r], recv_sem=face_recv.at[r],
+            device_id=across(r), device_id_type=MESH,
+        )
+
+    def halo_to(i):
+        return pltpu.make_async_remote_copy(
+            src_ref=edges.at[i], dst_ref=halos.at[i],
+            send_sem=halo_send.at[i], recv_sem=halo_recv.at[i],
+            device_id=(next_id, prev_id)[i], device_id_type=MESH,
+        )
+
     chunks = range(len(CHUNKS))
     for c in chunks:
         for d in ORDER:
             first(c, d).start()
     for copy in loads:
         copy.wait()
+
+    wide = lax.broadcasted_iota(jnp.int32, (ROWS, LANES), 1)
+    outward = coef[3]
+    columns = jnp.zeros((ROWS, LANES), jnp.float32)
+    for k in range(2 * NV):
+        n, u = divmod(k, NV)
+        columns = jnp.where(wide == k, pltpu.roll(outward * adj[n, u], k + 1, 1), columns)
+        edges[0, k : k + 1, :] = coef[1, ROWS - 1 : ROWS, :] * adj[n, u, ROWS - 1 : ROWS, :]
+        edges[1, k : k + 1, :] = coef[2, 0:1, :] * adj[n, u, 0:1, :]
+    payload[...] = columns.T[0:16, :]
+    for i in range(2):
+        edges[i, 2 * NV : 16, :] = jnp.zeros((16 - 2 * NV, LANES), jnp.float32)
+
+    def send_across(r, carry):
+        face_to(r).start()
+        return carry
+
+    lax.fori_loop(0, earlier, send_across, 0)
+    pl.when(next_earlier)(lambda: halo_to(0).start())
+    pl.when(prev_earlier)(lambda: halo_to(1).start())
 
     lane = lax.broadcasted_iota(jnp.int32, (BLK, LANES), 1)
 
@@ -176,6 +229,54 @@
         for d in ORDER:
             second(c, d).start()
 
+    def answer_across(r, carry):
+        face_from(r).wait_recv()
+        face_to(r).start()
+        return carry
+
+    def answer_next():
+        halo_to(1).wait_recv()
+        halo_to(0).start()
+
+    def answer_prev():
+        halo_to(0).wait_recv()
+        halo_to(1).start()
+
+    pl.when(jnp.logical_not(next_earlier))(answer_next)
+    pl.when(jnp.logical_not(prev_earlier))(answer_prev)
+    lax.fori_loop(earlier, SECTORS, answer_across, 0)
+
+    def take_across(r, carry):
+        face_from(r).wait_recv()
+        return carry
+
+    pl.when(next_earlier)(lambda: halo_to(1).wait_recv())
+    pl.when(prev_earlier)(lambda: halo_to(0).wait_recv())
+    lax.fori_loop(0, earlier, take_across, 0)
+
+    thin = lax.broadcasted_iota(jnp.int32, (16, LANES), 1) // FB
+    mixed = []
+    for n in range(2):
+        rows = jnp.zeros((16, LANES), jnp.float32)
+        for b in range(NB):
+            block = partner[n, NB * p + b]
+            sector, kind = block // (2 * NB), lax.rem(block, NB)
+            face = faces[lax.rem(sector, NZ) * NX + sector // NZ]
+            for turn in range(NB):
+                here = jnp.logical_and(thin == b, kind == (b - turn) % NB)
+                rows = jnp.where(here, pltpu.roll(face, turn * FB, 1) if turn else face, rows)
+        for v in range(NV):
+            mixed.append(sum(mixing[3, u, v] * rows[n * NV + u : n * NV + u + 1, :] for u in range(NV)))
+    mixed = jnp.concatenate(mixed + [jnp.zeros((LANES - 2 * NV, LANES), jnp.float32)], axis=0).T
+    for k in range(2 * NV):
+        n, v = divmod(k, NV)
+        column = pltpu.roll(mixed, LANES - 1 - k, 1)
+        base[n, v] = base[n, v] + jnp.where(wide == LANES - 1, column, 0.0)
+        first_row = sum(mixing[1, u, v] * halos[0, n * NV + u : n * NV + u + 1, :] for u in range(NV))
+        last_row = sum(mixing[2, u, v] * halos[1, n * NV + u : n * NV + u + 1, :] for u in range(NV))
+        base[n, v, 0:1, :] = base[n, v, 0:1, :] + first_row
+        base[n, v, ROWS - 1 : ROWS, :] = base[n, v, ROWS - 1 : ROWS, :] + last_row
+
     stores = []
     for c in chunks:
         v0, nv = CHUNKS[c]
@@ -198,94 +299,48 @@
         for d in ORDER:
             first(c, d).wait_send()
             second(c, d).wait_send()
+
+    def sent_across(r, carry):
+        face_to(r).wait_send()
+        return carry
+
+    lax.fori_loop(0, SECTORS, sent_across, 0)
+    for i in range(2):
+        halo_to(i).wait_send()
     for store in stores:
         store.wait()
 
 
-def last_kernel(part, received, mixing, partner, out, halo, face, sems):
-    p = lax.axis_index("space")
-    count = 64
-    copies = [
-        pltpu.make_async_copy(received.at[lax.rem(p + count - 2, count)], halo.at[0], sems.at[8]),
-        pltpu.make_async_copy(received.at[lax.rem(p + 2, count)], halo.at[1], sems.at[9]),
-    ]
-    shifts = []
-    for n in range(2):
-        for b in range(NB):
-            x = partner[n, NB * p + b]
-            shifts.append(lax.rem(b - lax.rem(x, NB) + NB, NB) * FB)
-            copies.append(
-                pltpu.make_async_copy(received.at[x // NB, pl.ds(0, 16)], face.at[n * NB + b], sems.at[n * NB + b])
-            )
-    for copy in copies:
-        copy.start()
-    for copy in copies:
-        copy.wait()
-    lane = lax.broadcasted_iota(jnp.int32, (16, LANES), 1)
-    mixed = []
-    for n in range(2):
-        rows = jnp.zeros((16, LANES), jnp.float32)
-        for b in range(NB):
-            rows = jnp.where(lane // FB == b, pltpu.roll(face[n * NB + b], shifts[n * NB + b], 1), rows)
-        for v in range(NV):
-            mixed.append(sum(mixing[3, u, v] * rows[n * NV + u : n * NV + u + 1, :] for u in range(NV)))
-    mixed = jnp.concatenate(mixed + [jnp.zeros((LANES - 2 * NV, LANES), jnp.float32)], axis=0).T
-    wide = lax.broadcasted_iota(jnp.int32, (ROWS, LANES), 1)
-    for k in range(2 * NV):
-        n, v = divmod(k, NV)
-        column = pltpu.roll(mixed, LANES - 1 - k, 1)
-        out[n, v] = part[n, v] + jnp.where(wide == LANES - 1, column, 0.0)
-        first = sum(mixing[1, u, v] * halo[0, 10 + n * NV + u : 11 + n * NV + u, :] for u in range(NV))
-        last = sum(mixing[2, u, v] * halo[1, 20 + n * NV + u : 21 + n * NV + u, :] for u in range(NV))
-        out[n, v, 0:1, :] = out[n, v, 0:1, :] + first
-        out[n, v, ROWS - 1 : ROWS, :] = out[n, v, ROWS - 1 : ROWS, :] + last
-
-
 def local(adjoint, source, coefficient, volume, mixing, face_partner):
     f32 = jnp.float32
-    vmem, smem, anywhere = (pl.BlockSpec(memory_space=s) for s in (pltpu.VMEM, pltpu.SMEM, pl.ANY))
-    payload = pl.pallas_call(
-        payload_kernel,
-        out_shape=jax.ShapeDtypeStruct((32, LANES), f32),
-        in_specs=[vmem, vmem],
-        out_specs=vmem,
-        name="payload",
-    )(adjoint, coefficient)
-    received = lax.all_gather(payload, "space")
+    smem, hbm = pl.BlockSpec(memory_space=pltpu.SMEM), pl.BlockSpec(memory_space=pltpu.HBM)
     shard = (2, NV, ROWS, LANES)
     nc = len(CHUNKS)
-    part = pl.pallas_call(
+    return pl.pallas_call(
         main_kernel,
         out_shape=jax.ShapeDtypeStruct(shard, f32),
-        in_specs=[anywhere, anywhere, anywhere, anywhere, smem, anywhere],
-        out_specs=anywhere,
+        in_specs=[hbm, hbm, hbm, hbm, smem, smem],
+        out_specs=hbm,
         scratch_shapes=[
             pltpu.VMEM(shard, f32), pltpu.VMEM(shard, f32),
             pltpu.VMEM((5, ROWS, LANES), f32), pltpu.VMEM((ROWS, LANES), f32),
             pltpu.VMEM(shard, f32), pltpu.VMEM(shard, f32),
             pltpu.VMEM((ND, 2, NV, BLK, LANES), f32), pltpu.VMEM((ND, 2, NV, BLK, LANES), f32),
             pltpu.VMEM(shard, f32),
+            pltpu.VMEM((16, LANES), f32), pltpu.VMEM((SECTORS, 16, LANES), f32),
+            pltpu.VMEM((2, 16, LANES), f32), pltpu.VMEM((2, 16, LANES), f32),
             pltpu.SemaphoreType.DMA((4,)), pltpu.SemaphoreType.DMA((nc,)),
             pltpu.SemaphoreType.DMA((nc, ND)), pltpu.SemaphoreType.DMA((nc, ND)),
             pltpu.SemaphoreType.DMA((nc, ND)), pltpu.SemaphoreType.DMA((nc, ND)),
+            pltpu.SemaphoreType.DMA((SECTORS,)), pltpu.SemaphoreType.DMA((SECTORS,)),
+            pltpu.SemaphoreType.DMA((2,)), pltpu.SemaphoreType.DMA((2,)),
         ],
         compiler_params=pltpu.CompilerParams(
             collective_id=0, has_side_effects=True, vmem_limit_bytes=VMEM_LIMIT
         ),
         cost_estimate=pl.CostEstimate(flops=20_000_000, bytes_accessed=60_000_000, transcendentals=0),
-        name="spectral_and_stencil",
-    )(adjoint, source, coefficient, volume, mixing, payload)
-    return pl.pallas_call(
-        last_kernel,
-        out_shape=jax.ShapeDtypeStruct(shard, f32),
-        in_specs=[vmem, anywhere, smem, smem],
-        out_specs=vmem,
-        scratch_shapes=[
-            pltpu.VMEM((2, 32, LANES), f32), pltpu.VMEM((2 * NB, 16, LANES), f32),
-            pltpu.SemaphoreType.DMA((10,)),
-        ],
-        name="boundaries",
-    )(part, received, mixing, face_partner)
+        name="residual",
+    )(adjoint, source, coefficient, volume, mixing, face_partner)
 
 
 def solution(mesh):

time: 110 us -> 42 us (0.38)
  the two profiles are of different devices: /device:TPU:1 before, /device:TPU:449 now
where the time goes in v2:
time: 42 us; the launch traced here: 41.7 us
  Pallas kernels  39.7 us (95%)
  local copies, waits for them, and re-layouts  1.97 us (5%)
    pallas_call x1, Pallas kernels, local(): pl.pallas_call(main_kernel, out_shape=jax.ShapeDtypeStruct(shard, f32), i...  39.7 us
    unnamed x1, local copies, waits for them, and re-layouts  1.97 us

profile of v2, /device:TPU:449, one launch (start us, length us, event | category | flops | bytes accessed | tf_op | source)
XLA Modules:
  0.0 41.7 jit_solution(12951785733953488932)
XLA Ops:
  0.0 39.7 %residual.1 = f32[2,5,128,128]{3,2,1,0:T(8,128)} custom-call(f32[2,5,128,128]{3,2,1,0:T(8,128)} %adj_hbm.1, f32[2,5,128,128]{3,2,1,0:T(8,128)} %src_hbm.1, f32[5,128,128]{2,1,0:T(8,128)} %coef_hbm.1, f32[128,128]{1,0:T(8,128)} %vol_hbm.1, f32[5,5,5]{2,1,0:T(8,128)} %mixing.1, s32[2,256]{1,0:T(2,128)} %partner.1), custom_call_target="tpu_custom_call" | custom-call | flops 20000000 | bytes 60000000 | tf_op jit(solution)/shard_map/residual/pallas_call | solution.py:319
  39.8 2.0 %copy.8 = f32[2,5,128,128]{3,2,1,0:T(8,128)} copy(f32[2,5,128,128]{3,2,1,0:T(8,128)} %residual.1) | data formatting | bytes 1310720

commit v3 on v2

--- a/solution.py
+++ b/solution.py
@@ -25,7 +25,7 @@
 SPIN_RATE = 0.75
 CHUNKS = ((0, 3), (3, 2))
 ORDER = (4, 3, 5, 2, 6, 1, 7)
-VMEM_LIMIT = 56 * 1024 * 1024
+VMEM_LIMIT = 16 * 1024 * 1024
 
 
 def spectral_entries():
@@ -36,8 +36,9 @@
 
 
 def main_kernel(
-    adj_hbm, src_hbm, coef_hbm, vol_hbm, mixing, partner, out_hbm,
+    adj_hbm, src_hbm, coef_hbm, vol_hbm, mixing_hbm, partner_hbm, out_hbm,
     adj, base, coef, vol, ahead, behind, gathered, turned, spectral, payload, faces, edges, halos,
+    mixing, partner,
     load_sem, store_sem, send1, recv1, send2, recv2, face_send, face_recv, halo_send, halo_recv,
 ):
     me = lax.axis_index("inst")
@@ -70,7 +71,10 @@
     pl.when(jnp.logical_not(prev_earlier))(lambda: greet(prev_id))
     loads = [
         pltpu.make_async_copy(s, t, load_sem.at[i])
-        for i, (s, t) in enumerate(((adj_hbm, adj), (coef_hbm, coef), (src_hbm, base), (vol_hbm, vol)))
+        for i, (s, t) in enumerate((
+            (adj_hbm, adj), (coef_hbm, coef), (src_hbm, base), (vol_hbm, vol),
+            (mixing_hbm, mixing), (partner_hbm, partner),
+        ))
     ]
     for copy in loads:
         copy.start()
@@ -313,13 +317,15 @@
 
 def local(adjoint, source, coefficient, volume, mixing, face_partner):
     f32 = jnp.float32
-    smem, hbm = pl.BlockSpec(memory_space=pltpu.SMEM), pl.BlockSpec(memory_space=pltpu.HBM)
+    hbm = pl.BlockSpec(memory_space=pltpu.HBM)
     shard = (2, NV, ROWS, LANES)
     nc = len(CHUNKS)
+    given = (adjoint, source, coefficient, volume, mixing, face_partner)
+    operands = [pltpu.with_memory_space_constraint(t, pltpu.HBM) for t in given]
     return pl.pallas_call(
         main_kernel,
         out_shape=jax.ShapeDtypeStruct(shard, f32),
-        in_specs=[hbm, hbm, hbm, hbm, smem, smem],
+        in_specs=[hbm] * 6,
         out_specs=hbm,
         scratch_shapes=[
             pltpu.VMEM(shard, f32), pltpu.VMEM(shard, f32),
@@ -329,7 +335,8 @@
             pltpu.VMEM(shard, f32),
             pltpu.VMEM((16, LANES), f32), pltpu.VMEM((SECTORS, 16, LANES), f32),
             pltpu.VMEM((2, 16, LANES), f32), pltpu.VMEM((2, 16, LANES), f32),
-            pltpu.SemaphoreType.DMA((4,)), pltpu.SemaphoreType.DMA((nc,)),
+            pltpu.SMEM((5, NV, NV), f32), pltpu.SMEM((2, SECTORS * 2 * NB), jnp.int32),
+            pltpu.SemaphoreType.DMA((6,)), pltpu.SemaphoreType.DMA((nc,)),
             pltpu.SemaphoreType.DMA((nc, ND)), pltpu.SemaphoreType.DMA((nc, ND)),
             pltpu.SemaphoreType.DMA((nc, ND)), pltpu.SemaphoreType.DMA((nc, ND)),
             pltpu.SemaphoreType.DMA((SECTORS,)), pltpu.SemaphoreType.DMA((SECTORS,)),
@@ -340,7 +347,7 @@
         ),
         cost_estimate=pl.CostEstimate(flops=20_000_000, bytes_accessed=60_000_000, transcendentals=0),
         name="residual",
-    )(adjoint, source, coefficient, volume, mixing, face_partner)
+    )(*operands)
 
 
 def solution(mesh):

time: 42 us -> 39.3 us (0.936)
  Pallas kernels: 39.7 us -> 38.3 us
  local copies, waits for them, and re-layouts: 1.97 us -> 0.84 us
    pallas_call x1, Pallas kernels: 39.7 us -> 38.3 us  [local(): pl.pallas_call(main_kernel, out_shape=jax.ShapeDtypeStruct(shard, f32), i...]
    unnamed x1, local copies, waits for them, and re-layouts: 1.97 us -> 0.84 us
where the time goes in v3:
time: 39.3 us; the launch traced here: 39.1 us
  Pallas kernels  38.3 us (97%)
  local copies, waits for them, and re-layouts  0.84 us (2%)
    pallas_call x1, Pallas kernels, local(): pl.pallas_call(main_kernel, out_shape=jax.ShapeDtypeStruct(shard, f32), i...  38.3 us
    unnamed x1, local copies, waits for them, and re-layouts  0.84 us

profile of v3, /device:TPU:449, one launch (start us, length us, event | category | flops | bytes accessed | tf_op | source)
XLA Modules:
  0.0 39.1 jit_solution(7983163823507782521)
XLA Ops:
  0.0 38.3 %residual.1 = f32[2,5,128,128]{3,2,1,0:T(8,128)S(1)} custom-call(f32[2,5,128,128]{3,2,1,0:T(8,128)} %adj_hbm.1, f32[2,5,128,128]{3,2,1,0:T(8,128)} %src_hbm.1, f32[5,128,128]{2,1,0:T(8,128)} %coef_hbm.1, f32[128,128]{1,0:T(8,128)} %vol_hbm.1, f32[5,5,5]{2,1,0:T(8,128)} %mixing_hbm.1, s32[2,256]{1,0:T(2,128)} %partner_hbm.1), custom_call_target="tpu_custom_call" | custom-call | flops 20000000 | bytes 60000000 | tf_op jit(solution)/shard_map/residual/pallas_call | solution.py:325
  38.3 0.8 %copy.8 = f32[2,5,128,128]{3,2,1,0:T(8,128)} copy(f32[2,5,128,128]{3,2,1,0:T(8,128)S(1)} %residual.1) | data formatting | bytes 1310720

commit v4 on v3

--- a/solution.py
+++ b/solution.py
@@ -39,34 +39,43 @@
     adj_hbm, src_hbm, coef_hbm, vol_hbm, mixing_hbm, partner_hbm, out_hbm,
     adj, base, coef, vol, ahead, behind, gathered, turned, spectral, payload, faces, edges, halos,
     mixing, partner,
-    load_sem, store_sem, send1, recv1, send2, recv2, face_send, face_recv, halo_send, halo_recv,
+    load_sem, store_sem, send1, recv1, send2, recv2, face_send, face_recv, halo_send, halo_recv, heard, column_in, columns_in, all_in,
 ):
     me = lax.axis_index("inst")
     p = lax.axis_index("space")
     side = lax.rem(p, 2)
     z, x = lax.rem(p // 2, NZ), p // (2 * NZ)
-    rank = z * NX + x
-    earlier = rank + 1 - side
+    sector = x * NZ + z
+    is_hub = z == 0
+    is_chief = jnp.logical_and(is_hub, jnp.logical_and(x == 0, side == 1))
     next_earlier, prev_earlier = z == NZ - 1, z != 0
     next_id = {"space": lax.rem(p + 2, SPACE)}
     prev_id = {"space": lax.rem(p + SPACE - 2, SPACE)}
 
-    def across(r):
-        return {"space": 2 * (lax.rem(r, NX) * NZ + r // NX) + 1 - side}
+    def at(x, z, side):
+        return {"space": 2 * (x * NZ + z) + side}
+
+    def over_hubs(act):
+        for other in range(NX):
+            if other:
+                act(at(other, 0, 1))
+            act(at(other, 0, 0))
+
+    def over_column(act):
+        for other in range(1, NZ):
+            act(at(x, other, side))
 
     barrier = pltpu.get_barrier_semaphore()
 
     def greet(device):
         pl.semaphore_signal(barrier, inc=1, device_id=device, device_id_type=MESH)
 
-    for d in range(1, ND):
-        greet({"inst": lax.rem(me + d, ND)})
-
-    def greet_across(r, carry):
-        greet(across(r))
-        return carry
-
-    lax.fori_loop(earlier, SECTORS, greet_across, 0)
+    up, down = {"inst": lax.rem(me + 1, ND)}, {"inst": lax.rem(me + ND - 1, ND)}
+    greet(up)
+    greet(down)
+
+    pl.when(is_chief)(lambda: over_hubs(greet))
+    pl.when(is_hub)(lambda: over_column(greet))
     pl.when(jnp.logical_not(next_earlier))(lambda: greet(next_id))
     pl.when(jnp.logical_not(prev_earlier))(lambda: greet(prev_id))
     loads = [
@@ -78,7 +87,8 @@
     ]
     for copy in loads:
         copy.start()
-    pl.semaphore_wait(barrier, ND - 1 + earlier + next_earlier.astype(jnp.int32) + prev_earlier.astype(jnp.int32))
+    greetings = jnp.where(is_hub, 1 - is_chief.astype(jnp.int32), 2 + next_earlier.astype(jnp.int32))
+    pl.semaphore_wait(barrier, 2 + greetings)
 
     my_rows = pl.ds(pl.multiple_of(me * BLK, BLK), BLK)
 
@@ -102,18 +112,18 @@
             device_id={"inst": to}, device_id_type=MESH,
         )
 
-    def face_to(r):
+    def face_to(other):
         return pltpu.make_async_remote_copy(
-            src_ref=payload, dst_ref=faces.at[rank],
-            send_sem=face_send.at[r], recv_sem=face_recv.at[rank],
-            device_id=across(r), device_id_type=MESH,
-        )
-
-    def face_from(r):
+            src_ref=payload, dst_ref=faces.at[sector],
+            send_sem=face_send.at[other], recv_sem=face_recv.at[sector],
+            device_id={"space": 2 * other + 1 - side}, device_id_type=MESH,
+        )
+
+    def face_from(other):
         return pltpu.make_async_remote_copy(
-            src_ref=payload, dst_ref=faces.at[r],
-            send_sem=face_send.at[r], recv_sem=face_recv.at[r],
-            device_id=across(r), device_id_type=MESH,
+            src_ref=payload, dst_ref=faces.at[other],
+            send_sem=face_send.at[other], recv_sem=face_recv.at[other],
+            device_id={"space": 2 * other + 1 - side}, device_id_type=MESH,
         )
 
     def halo_to(i):
@@ -124,7 +134,35 @@
         )
 
     chunks = range(len(CHUNKS))
-    for c in chunks:
+
+    def heard_of(i):
+        pl.semaphore_wait(heard.at[i], 1)
+
+    def signal(semaphore, device):
+        pl.semaphore_signal(semaphore, inc=1, device_id=device, device_id_type=MESH)
+
+    def tell(device, i):
+        signal(heard.at[i], device)
+
+    tell(down, 0)
+    tell(up, 1)
+    first(0, 1).start()
+    first(0, ND - 1).start()
+    heard_of(0)
+    tell(down, 2)
+    first(0, 2).start()
+    heard_of(1)
+    tell(up, 3)
+    first(0, ND - 2).start()
+    heard_of(2)
+    tell(down, 4)
+    first(0, 3).start()
+    heard_of(3)
+    first(0, ND - 3).start()
+    heard_of(4)
+    first(0, 4).start()
+    pl.when(jnp.logical_not(is_hub))(lambda: signal(column_in, at(x, 0, side)))
+    for c in chunks[1:]:
         for d in ORDER:
             first(c, d).start()
     for copy in loads:
@@ -138,15 +176,8 @@
         columns = jnp.where(wide == k, pltpu.roll(outward * adj[n, u], k + 1, 1), columns)
         edges[0, k : k + 1, :] = coef[1, ROWS - 1 : ROWS, :] * adj[n, u, ROWS - 1 : ROWS, :]
         edges[1, k : k + 1, :] = coef[2, 0:1, :] * adj[n, u, 0:1, :]
-    payload[...] = columns.T[0:16, :]
-    for i in range(2):
-        edges[i, 2 * NV : 16, :] = jnp.zeros((16 - 2 * NV, LANES), jnp.float32)
-
-    def send_across(r, carry):
-        face_to(r).start()
-        return carry
-
-    lax.fori_loop(0, earlier, send_across, 0)
+    payload[...] = columns.T[0 : 2 * NV, :]
+
     pl.when(next_earlier)(lambda: halo_to(0).start())
     pl.when(prev_earlier)(lambda: halo_to(1).start())
 
@@ -190,6 +221,26 @@
         return carry
 
     lax.fori_loop(0, 2 * NV, moved, 0)
+
+    def report():
+        pl.semaphore_wait(column_in, NZ - 1)
+        pl.when(jnp.logical_not(is_chief))(lambda: signal(columns_in, at(0, 0, 1)))
+
+    def spread():
+        pl.semaphore_wait(columns_in, 2 * NX - 1)
+        over_hubs(lambda device: signal(all_in, device))
+
+    def send_faces():
+        pl.when(jnp.logical_not(is_chief))(lambda: pl.semaphore_wait(all_in, 1))
+        pl.when(is_hub)(lambda: over_column(lambda device: signal(all_in, device)))
+
+        def send_face(other, carry):
+            face_to(other).start()
+            return carry
+
+        lax.fori_loop(0, SECTORS, send_face, 0)
+
+    pl.when(is_hub)(report)
 
     entries = spectral_entries()
     half = NI // 2
@@ -232,11 +283,9 @@
         transform(c)
         for d in ORDER:
             second(c, d).start()
-
-    def answer_across(r, carry):
-        face_from(r).wait_recv()
-        face_to(r).start()
-        return carry
+        if c == 0:
+            pl.when(is_chief)(spread)
+            send_faces()
 
     def answer_next():
         halo_to(1).wait_recv()
@@ -248,24 +297,23 @@
 
     pl.when(jnp.logical_not(next_earlier))(answer_next)
     pl.when(jnp.logical_not(prev_earlier))(answer_prev)
-    lax.fori_loop(earlier, SECTORS, answer_across, 0)
-
-    def take_across(r, carry):
-        face_from(r).wait_recv()
-        return carry
 
     pl.when(next_earlier)(lambda: halo_to(1).wait_recv())
     pl.when(prev_earlier)(lambda: halo_to(0).wait_recv())
-    lax.fori_loop(0, earlier, take_across, 0)
-
-    thin = lax.broadcasted_iota(jnp.int32, (16, LANES), 1) // FB
+
+    def take_face(other, carry):
+        face_from(other).wait_recv()
+        return carry
+
+    lax.fori_loop(0, SECTORS, take_face, 0)
+
+    thin = lax.broadcasted_iota(jnp.int32, (2 * NV, LANES), 1) // FB
     mixed = []
     for n in range(2):
-        rows = jnp.zeros((16, LANES), jnp.float32)
+        rows = jnp.zeros((2 * NV, LANES), jnp.float32)
         for b in range(NB):
             block = partner[n, NB * p + b]
-            sector, kind = block // (2 * NB), lax.rem(block, NB)
-            face = faces[lax.rem(sector, NZ) * NX + sector // NZ]
+            face, kind = faces[block // (2 * NB)], lax.rem(block, NB)
             for turn in range(NB):
                 here = jnp.logical_and(thin == b, kind == (b - turn) % NB)
                 rows = jnp.where(here, pltpu.roll(face, turn * FB, 1) if turn else face, rows)
@@ -304,11 +352,11 @@
             first(c, d).wait_send()
             second(c, d).wait_send()
 
-    def sent_across(r, carry):
-        face_to(r).wait_send()
+    def sent_face(other, carry):
+        face_to(other).wait_send()
         return carry
 
-    lax.fori_loop(0, SECTORS, sent_across, 0)
+    lax.fori_loop(0, SECTORS, sent_face, 0)
     for i in range(2):
         halo_to(i).wait_send()
     for store in stores:
@@ -333,14 +381,16 @@
             pltpu.VMEM(shard, f32), pltpu.VMEM(shard, f32),
             pltpu.VMEM((ND, 2, NV, BLK, LANES), f32), pltpu.VMEM((ND, 2, NV, BLK, LANES), f32),
             pltpu.VMEM(shard, f32),
-            pltpu.VMEM((16, LANES), f32), pltpu.VMEM((SECTORS, 16, LANES), f32),
-            pltpu.VMEM((2, 16, LANES), f32), pltpu.VMEM((2, 16, LANES), f32),
+            pltpu.VMEM((2 * NV, LANES), f32), pltpu.VMEM((SECTORS, 2 * NV, LANES), f32),
+            pltpu.VMEM((2, 2 * NV, LANES), f32), pltpu.VMEM((2, 2 * NV, LANES), f32),
             pltpu.SMEM((5, NV, NV), f32), pltpu.SMEM((2, SECTORS * 2 * NB), jnp.int32),
             pltpu.SemaphoreType.DMA((6,)), pltpu.SemaphoreType.DMA((nc,)),
             pltpu.SemaphoreType.DMA((nc, ND)), pltpu.SemaphoreType.DMA((nc, ND)),
             pltpu.SemaphoreType.DMA((nc, ND)), pltpu.SemaphoreType.DMA((nc, ND)),
             pltpu.SemaphoreType.DMA((SECTORS,)), pltpu.SemaphoreType.DMA((SECTORS,)),
             pltpu.SemaphoreType.DMA((2,)), pltpu.SemaphoreType.DMA((2,)),
+            pltpu.SemaphoreType.REGULAR((5,)),
+            pltpu.SemaphoreType.REGULAR, pltpu.SemaphoreType.REGULAR, pltpu.SemaphoreType.REGULAR,
         ],
         compiler_params=pltpu.CompilerParams(
             collective_id=0, has_side_effects=True, vmem_limit_bytes=VMEM_LIMIT

time: 39.3 us -> 37.5 us (0.954)
  the two profiles are of different devices: /device:TPU:449 before, /device:TPU:450 now
where the time goes in v4:
time: 37.5 us; the launch traced here: 37.4 us
  Pallas kernels  36.5 us (97%)
  local copies, waits for them, and re-layouts  0.84 us (2%)
    pallas_call x1, Pallas kernels, local(): pl.pallas_call(main_kernel, out_shape=jax.ShapeDtypeStruct(shard, f32), i...  36.5 us
    unnamed x1, local copies, waits for them, and re-layouts  0.84 us

profile of v4, /device:TPU:450, one launch (start us, length us, event | category | flops | bytes accessed | tf_op | source)
XLA Modules:
  0.0 37.4 jit_solution(13738668781922942828)
XLA Ops:
  0.0 36.5 %residual.1 = f32[2,5,128,128]{3,2,1,0:T(8,128)S(1)} custom-call(f32[2,5,128,128]{3,2,1,0:T(8,128)} %adj_hbm.1, f32[2,5,128,128]{3,2,1,0:T(8,128)} %src_hbm.1, f32[5,128,128]{2,1,0:T(8,128)} %coef_hbm.1, f32[128,128]{1,0:T(8,128)} %vol_hbm.1, f32[5,5,5]{2,1,0:T(8,128)} %mixing_hbm.1, s32[2,256]{1,0:T(2,128)} %partner_hbm.1), custom_call_target="tpu_custom_call" | custom-call | flops 20000000 | bytes 60000000 | tf_op jit(solution)/shard_map/residual/pallas_call | solution.py:373
  36.5 0.8 %copy.8 = f32[2,5,128,128]{3,2,1,0:T(8,128)} copy(f32[2,5,128,128]{3,2,1,0:T(8,128)S(1)} %residual.1) | data formatting | bytes 1310720

commit v5 on v4

--- a/solution.py
+++ b/solution.py
@@ -23,6 +23,7 @@
 ROWS = 128
 LANES = 128
 SPIN_RATE = 0.75
+KNOWN = {4: (0, 1, 2), 5: (0, 1), 6: (0, 1), 7: (1,), 3: (0,)}
 CHUNKS = ((0, 3), (3, 2))
 ORDER = (4, 3, 5, 2, 6, 1, 7)
 VMEM_LIMIT = 16 * 1024 * 1024
@@ -73,6 +74,15 @@
     up, down = {"inst": lax.rem(me + 1, ND)}, {"inst": lax.rem(me + ND - 1, ND)}
     greet(up)
     greet(down)
+    for early in range(ND):
+        later = [late for late in KNOWN if early in KNOWN[late]]
+        if later:
+
+            @pl.when(me == early)
+            def greet_later(later=later):
+                for late in later:
+                    greet({"inst": late})
+
 
     pl.when(is_chief)(lambda: over_hubs(greet))
     pl.when(is_hub)(lambda: over_column(greet))
@@ -88,6 +98,8 @@
     for copy in loads:
         copy.start()
     greetings = jnp.where(is_hub, 1 - is_chief.astype(jnp.int32), 2 + next_earlier.astype(jnp.int32))
+    for late in KNOWN:
+        greetings = greetings + jnp.where(me == late, len(KNOWN[late]), 0)
     pl.semaphore_wait(barrier, 2 + greetings)
 
     my_rows = pl.ds(pl.multiple_of(me * BLK, BLK), BLK)
@@ -144,23 +156,37 @@
     def tell(device, i):
         signal(heard.at[i], device)
 
+    def unless_known(d):
+        known = me == -1
+        for late in KNOWN:
+            if (late + d) % ND in KNOWN[late]:
+                known = jnp.logical_or(known, me == late)
+        pl.when(jnp.logical_not(known))(lambda: first(0, d).start())
+
     tell(down, 0)
     tell(up, 1)
     first(0, 1).start()
     first(0, ND - 1).start()
+    for late in KNOWN:
+
+        @pl.when(me == late)
+        def send_known(late=late):
+            for early in KNOWN[late]:
+                first(0, (early - late) % ND).start()
+
     heard_of(0)
     tell(down, 2)
-    first(0, 2).start()
+    unless_known(2)
     heard_of(1)
     tell(up, 3)
-    first(0, ND - 2).start()
+    unless_known(ND - 2)
     heard_of(2)
     tell(down, 4)
-    first(0, 3).start()
+    unless_known(3)
     heard_of(3)
-    first(0, ND - 3).start()
+    unless_known(ND - 3)
     heard_of(4)
-    first(0, 4).start()
+    unless_known(4)
     pl.when(jnp.logical_not(is_hub))(lambda: signal(column_in, at(x, 0, side)))
     for c in chunks[1:]:
         for d in ORDER:
@@ -281,8 +307,19 @@
         for d in ORDER:
             first(c, d).wait_recv()
         transform(c)
-        for d in ORDER:
-            second(c, d).start()
+        to_first = lax.rem(ND - me, ND)
+        if c:
+            pl.when(to_first != 0)(lambda: second(c, to_first).start())
+        for core, order in enumerate(((4, 5, 3, 6, 2, 7, 1), (7, 1, 6, 2, 5, 3, 4))):
+
+            @pl.when(side == core)
+            def send_back(c=c, order=order):
+                for d in order:
+                    if c:
+                        pl.when(to_first != d)(lambda d=d: second(c, d).start())
+                    else:
+                        second(c, d).start()
+
         if c == 0:
             pl.when(is_chief)(spread)
             send_faces()

time: 37.5 us -> 37.2 us (level)
  the two profiles are of different devices: /device:TPU:450 before, /device:TPU:8 now
where the time goes in v5:
time: 37.2 us; the launch traced here: 37.1 us
  Pallas kernels  36.3 us (98%)
  local copies, waits for them, and re-layouts  0.84 us (2%)
    pallas_call x1, Pallas kernels, local(): pl.pallas_call(main_kernel, out_shape=jax.ShapeDtypeStruct(shard, f32), i...  36.3 us
    unnamed x1, local copies, waits for them, and re-layouts  0.84 us

profile of v5, /device:TPU:8, one launch (start us, length us, event | category | flops | bytes accessed | tf_op | source)
XLA Modules:
  0.0 37.1 jit_solution(14751517414202591533)
XLA Ops:
  0.0 36.3 %residual.1 = f32[2,5,128,128]{3,2,1,0:T(8,128)S(1)} custom-call(f32[2,5,128,128]{3,2,1,0:T(8,128)} %adj_hbm.1, f32[2,5,128,128]{3,2,1,0:T(8,128)} %src_hbm.1, f32[5,128,128]{2,1,0:T(8,128)} %coef_hbm.1, f32[128,128]{1,0:T(8,128)} %vol_hbm.1, f32[5,5,5]{2,1,0:T(8,128)} %mixing_hbm.1, s32[2,256]{1,0:T(2,128)} %partner_hbm.1), custom_call_target="tpu_custom_call" | custom-call | flops 20000000 | bytes 60000000 | tf_op jit(solution)/shard_map/residual/pallas_call | solution.py:410
  36.3 0.8 %copy.8 = f32[2,5,128,128]{3,2,1,0:T(8,128)} copy(f32[2,5,128,128]{3,2,1,0:T(8,128)S(1)} %residual.1) | data formatting | bytes 1310720

commit v6 on v5

--- a/solution.py
+++ b/solution.py
@@ -37,10 +37,10 @@
 
 
 def main_kernel(
-    adj_hbm, src_hbm, coef_hbm, vol_hbm, mixing_hbm, partner_hbm, out_hbm,
+    adj_hbm, src_hbm, coef_hbm, vol_hbm, mixing_hbm, partner_hbm, out,
     adj, base, coef, vol, ahead, behind, gathered, turned, spectral, payload, faces, edges, halos,
     mixing, partner,
-    load_sem, store_sem, send1, recv1, send2, recv2, face_send, face_recv, halo_send, halo_recv, heard, column_in, columns_in, all_in,
+    load_sem, send1, recv1, send2, recv2, face_send, face_recv, halo_send, halo_recv, heard, column_in, columns_in, all_in,
 ):
     me = lax.axis_index("inst")
     p = lax.axis_index("space")
@@ -366,7 +366,6 @@
         base[n, v, 0:1, :] = base[n, v, 0:1, :] + first_row
         base[n, v, ROWS - 1 : ROWS, :] = base[n, v, ROWS - 1 : ROWS, :] + last_row
 
-    stores = []
     for c in chunks:
         v0, nv = CHUNKS[c]
         for d in ORDER:
@@ -375,15 +374,10 @@
         def finish(step, carry, v0=v0):
             v = v0 + step // 2
             n = lax.rem(step, 2)
-            base[n, v] = base[n, v] + (SPIN_RATE * vol[...]) * spectral[n, v]
+            out[n, v] = base[n, v] + (SPIN_RATE * vol[...]) * spectral[n, v]
             return carry
 
         lax.fori_loop(0, 2 * nv, finish, 0)
-        store = pltpu.make_async_copy(
-            base.at[:, pl.ds(v0, nv)], out_hbm.at[:, pl.ds(v0, nv)], store_sem.at[c]
-        )
-        store.start()
-        stores.append(store)
     for c in chunks:
         for d in ORDER:
             first(c, d).wait_send()
@@ -396,8 +390,6 @@
     lax.fori_loop(0, SECTORS, sent_face, 0)
     for i in range(2):
         halo_to(i).wait_send()
-    for store in stores:
-        store.wait()
 
 
 def local(adjoint, source, coefficient, volume, mixing, face_partner):
@@ -411,7 +403,7 @@
         main_kernel,
         out_shape=jax.ShapeDtypeStruct(shard, f32),
         in_specs=[hbm] * 6,
-        out_specs=hbm,
+        out_specs=pl.BlockSpec(memory_space=pltpu.VMEM),
         scratch_shapes=[
             pltpu.VMEM(shard, f32), pltpu.VMEM(shard, f32),
             pltpu.VMEM((5, ROWS, LANES), f32), pltpu.VMEM((ROWS, LANES), f32),
@@ -421,7 +413,7 @@
             pltpu.VMEM((2 * NV, LANES), f32), pltpu.VMEM((SECTORS, 2 * NV, LANES), f32),
             pltpu.VMEM((2, 2 * NV, LANES), f32), pltpu.VMEM((2, 2 * NV, LANES), f32),
             pltpu.SMEM((5, NV, NV), f32), pltpu.SMEM((2, SECTORS * 2 * NB), jnp.int32),
-            pltpu.SemaphoreType.DMA((6,)), pltpu.SemaphoreType.DMA((nc,)),
+            pltpu.SemaphoreType.DMA((6,)),
             pltpu.SemaphoreType.DMA((nc, ND)), pltpu.SemaphoreType.DMA((nc, ND)),
             pltpu.SemaphoreType.DMA((nc, ND)), pltpu.SemaphoreType.DMA((nc, ND)),
             pltpu.SemaphoreType.DMA((SECTORS,)), pltpu.SemaphoreType.DMA((SECTORS,)),

time: 37.2 us -> 37.2 us (level)
  no operation moved by 1% of the time
where the time goes in v6:
time: 37.2 us; the launch traced here: 37.1 us
  Pallas kernels  36.2 us (97%)
  local copies, waits for them, and re-layouts  0.84 us (2%)
    pallas_call x1, Pallas kernels, local(): pl.pallas_call(main_kernel, out_shape=jax.ShapeDtypeStruct(shard, f32), i...  36.2 us
    unnamed x1, local copies, waits for them, and re-layouts  0.84 us

profile of v6, /device:TPU:8, one launch (start us, length us, event | category | flops | bytes accessed | tf_op | source)
XLA Modules:
  0.0 37.1 jit_solution(17017114777501711831)
XLA Ops:
  0.0 36.2 %residual.1 = f32[2,5,128,128]{3,2,1,0:T(8,128)S(1)} custom-call(f32[2,5,128,128]{3,2,1,0:T(8,128)} %adj_hbm.1, f32[2,5,128,128]{3,2,1,0:T(8,128)} %src_hbm.1, f32[5,128,128]{2,1,0:T(8,128)} %coef_hbm.1, f32[128,128]{1,0:T(8,128)} %vol_hbm.1, f32[5,5,5]{2,1,0:T(8,128)} %mixing_hbm.1, s32[2,256]{1,0:T(2,128)} %partner_hbm.1), custom_call_target="tpu_custom_call" | custom-call | flops 20000000 | bytes 60000000 | tf_op jit(solution)/shard_map/residual/pallas_call | solution.py:402
  36.2 0.8 %copy.8 = f32[2,5,128,128]{3,2,1,0:T(8,128)} copy(f32[2,5,128,128]{3,2,1,0:T(8,128)S(1)} %residual.1) | data formatting | bytes 1310720

commit v7 on v6

--- a/solution.py
+++ b/solution.py
@@ -309,13 +309,13 @@
         transform(c)
         to_first = lax.rem(ND - me, ND)
         if c:
-            pl.when(to_first != 0)(lambda: second(c, to_first).start())
+            pl.when(jnp.logical_and(side == 0, to_first != 0))(lambda: second(c, to_first).start())
         for core, order in enumerate(((4, 5, 3, 6, 2, 7, 1), (7, 1, 6, 2, 5, 3, 4))):
 
             @pl.when(side == core)
-            def send_back(c=c, order=order):
+            def send_back(c=c, core=core, order=order):
                 for d in order:
-                    if c:
+                    if c and core == 0:
                         pl.when(to_first != d)(lambda d=d: second(c, d).start())
                     else:
                         second(c, d).start()

time: 37.2 us -> 37.3 us (level)
  no operation moved by 1% of the time
where the time goes in v7:
time: 37.3 us; the launch traced here: 37.2 us
  Pallas kernels  36.3 us (97%)
  local copies, waits for them, and re-layouts  0.84 us (2%)
    pallas_call x1, Pallas kernels, local(): pl.pallas_call(main_kernel, out_shape=jax.ShapeDtypeStruct(shard, f32), i...  36.3 us
    unnamed x1, local copies, waits for them, and re-layouts  0.84 us

profile of v7, /device:TPU:8, one launch (start us, length us, event | category | flops | bytes accessed | tf_op | source)
XLA Modules:
  0.0 37.2 jit_solution(5937673139108546406)
XLA Ops:
  0.0 36.3 %residual.1 = f32[2,5,128,128]{3,2,1,0:T(8,128)S(1)} custom-call(f32[2,5,128,128]{3,2,1,0:T(8,128)} %adj_hbm.1, f32[2,5,128,128]{3,2,1,0:T(8,128)} %src_hbm.1, f32[5,128,128]{2,1,0:T(8,128)} %coef_hbm.1, f32[128,128]{1,0:T(8,128)} %vol_hbm.1, f32[5,5,5]{2,1,0:T(8,128)} %mixing_hbm.1, s32[2,256]{1,0:T(2,128)} %partner_hbm.1), custom_call_target="tpu_custom_call" | custom-call | flops 20000000 | bytes 60000000 | tf_op jit(solution)/shard_map/residual/pallas_call | solution.py:402
  36.4 0.8 %copy.8 = f32[2,5,128,128]{3,2,1,0:T(8,128)} copy(f32[2,5,128,128]{3,2,1,0:T(8,128)S(1)} %residual.1) | data formatting | bytes 1310720
